TPU v7x, 32 devices: a whole 2x2x4 slice. The times are simulated.
32 devices in a mesh: frame: 4 (over x, core), clip: 8 (over z, y).
Axes of the slice: x: 2, y: 2, z: 4, core: 2. Of those that a mesh axis runs over, the one named last changes fastest.
Arguments:
- tokens: bfloat16 [96, 320, 768], P('clip', 'frame'), may hold values from -6 to 6
- cotangent: bfloat16 [96, 320, 768], P('clip', 'frame'), may hold values from -6 to 6
- frame_count: int32 [96], P('clip'), may hold values from 1 to 8, as said below
- image_group: int32 [96, 8], P('clip', 'frame'), may hold values from 0 to 3
- keep_mask: int32 [96, 320], P('clip', 'frame'), may hold values from 0 to 1, as said below
- attn_norm_gain: bfloat16 [768], P(('frame', 'clip')), may hold values from 0.5 to 1.5
- attn_norm_bias: bfloat16 [768], P(('frame', 'clip')), may hold values from -1.5 to 1.5
- w_qkv: bfloat16 [768, 2304], P(('frame', 'clip')), may hold values from -0.21875 to 0.21875
- query_bias: bfloat16 [768], P(('frame', 'clip')), may hold values from -1.5 to 1.5
- value_bias: bfloat16 [768], P(('frame', 'clip')), may hold values from -1.5 to 1.5
- w_out: bfloat16 [768, 768], P(('frame', 'clip')), may hold values from -0.625 to 0.625
- out_bias: bfloat16 [768], P(('frame', 'clip')), may hold values from -1.5 to 1.5
- mlp_norm_gain: bfloat16 [768], P(('frame', 'clip')), may hold values from 0.5 to 1.5
- mlp_norm_bias: bfloat16 [768], P(('frame', 'clip')), may hold values from -1.5 to 1.5
- w_up: bfloat16 [768, 3072], P(('frame', 'clip')), may hold values from -0.21875 to 0.21875
- up_bias: bfloat16 [3072], P(('frame', 'clip')), may hold values from -1.5 to 1.5
- w_down: bfloat16 [3072, 768], P(('frame', 'clip')), may hold values from -0.109375 to 0.109375
- down_bias: bfloat16 [768], P(('frame', 'clip')), may hold values from -1.5 to 1.5
Outputs:
- output: bfloat16 [96, 320, 768], P('clip', 'frame')
- input_grad: float32 [96, 320, 768], P('clip', 'frame')
- grad_attn_norm_gain: float32 [768], P(('frame', 'clip'))
- grad_attn_norm_bias: float32 [768], P(('frame', 'clip'))
- grad_w_qkv: float32 [768, 2304], P(('frame', 'clip'))
- grad_query_bias: float32 [768], P(('frame', 'clip'))
- grad_value_bias: float32 [768], P(('frame', 'clip'))
- grad_w_out: float32 [768, 768], P(('frame', 'clip'))
- grad_out_bias: float32 [768], P(('frame', 'clip'))
- grad_mlp_norm_gain: float32 [768], P(('frame', 'clip'))
- grad_mlp_norm_bias: float32 [768], P(('frame', 'clip'))
- grad_w_up: float32 [768, 3072], P(('frame', 'clip'))
- grad_up_bias: float32 [3072], P(('frame', 'clip'))
- grad_w_down: float32 [3072, 768], P(('frame', 'clip'))
- grad_down_bias: float32 [768], P(('frame', 'clip'))
Inputs may be any that keep to these rules, and one draw needn't show every extreme that they name: The first frame_count frames of a slot are one clip, the others single images; in each aligned run of 12 slots one slot holds a clip of all 8 frames. `image_group`: entries of frames that belong to the clip are unused. `keep_mask`: every frame of every slot keeps at least one of its 40 positions.
All inputs are finite; a program needn't handle non-finite values.
Results may differ from a plain program's by a relative error of at most 0.012.
Values may be sent and summed in bfloat16 or wider, within the bound.
No kernel may reach another device: no remote copies, remote signals or barrier semaphores. Data moves between devices by JAX's collectives and lax.ppermute only.
A program may use at most 256 MiB of HBM per device.

v0:
```python
import jax
import jax.numpy as jnp
from jax import lax
from jax.sharding import PartitionSpec as P

HEADS = 12
SLOT_MB = 4
MICRO = 3


EPSILON = 1e-06


def layer_norm(values, gain, shift):
    center = values - jnp.mean(values, axis=-1, keepdims=True)
    spread = jnp.mean(center * center, axis=-1, keepdims=True)
    return center * lax.rsqrt(spread + EPSILON) * gain + shift


def gelu_exact(values):
    return jax.nn.gelu(values, approximate=False)


def raw_scores(query_rows, key_rows, segment_rows, code_rows):
    slot_count, length, model_width = query_rows.shape
    key_length = key_rows.shape[1]
    head_dim = model_width // HEADS
    query_heads = query_rows.reshape(slot_count, length, HEADS, head_dim)
    key_heads = key_rows.reshape(slot_count, key_length, HEADS, head_dim)
    scores = jnp.einsum(
        "sqhd,skhd->shqk", query_heads, key_heads, preferred_element_type=jnp.float32
    ) * head_dim ** (-0.5)
    allowed = segment_rows[:, None, :, None] == code_rows[:, None, None, :]
    return (scores, allowed)


def layer_step(full, token_rows, cotangent_rows, segment_rows, code_rows, kept_mask):
    (
        attn_gain,
        attn_shift,
        w_qkv,
        query_bias,
        value_bias,
        w_out,
        out_bias,
        mlp_gain,
        mlp_shift,
        w_up,
        up_bias,
        w_down,
        down_bias,
    ) = full
    attn_gain = attn_gain.astype(jnp.float32)
    attn_shift = attn_shift.astype(jnp.float32)
    mlp_gain = mlp_gain.astype(jnp.float32)
    mlp_shift = mlp_shift.astype(jnp.float32)
    slot_count, length, model_width = token_rows.shape
    row_count = slot_count * length
    head_dim = model_width // HEADS
    block_shape = (slot_count, length, model_width)
    inputs = token_rows.reshape(row_count, model_width).astype(jnp.float32)
    first_low = layer_norm(inputs, attn_gain, attn_shift).astype(jnp.bfloat16)
    projected = jnp.dot(first_low, w_qkv, preferred_element_type=jnp.float32)
    query_rows = (
        (projected[:, :model_width] + query_bias.astype(jnp.float32))
        .astype(jnp.bfloat16)
        .reshape(block_shape)
    )
    key_rows = projected[:, model_width : 2 * model_width].astype(jnp.bfloat16).reshape(block_shape)
    value_rows = (
        (projected[:, 2 * model_width :] + value_bias.astype(jnp.float32))
        .astype(jnp.bfloat16)
        .reshape(block_shape)
    )
    key_all, value_all, code_all = (
        lax.all_gather(key_rows, "frame", axis=1, tiled=True),
        lax.all_gather(value_rows, "frame", axis=1, tiled=True),
        lax.all_gather(code_rows, "frame", axis=1, tiled=True),
    )
    key_length = key_all.shape[1]
    scores, allowed = raw_scores(query_rows, key_all, segment_rows, code_all)
    masked = jnp.where(allowed, scores, -1e30)
    row_max = jnp.max(masked, axis=-1, keepdims=True)
    weights = jnp.where(allowed, jnp.exp(masked - row_max), 0.0)
    total = jnp.sum(weights, axis=-1, keepdims=True)
    log_total = row_max + jnp.log(total)
    probability = (weights / total).astype(jnp.bfloat16)
    value_heads = value_all.reshape(slot_count, key_length, HEADS, head_dim)
    attended = jnp.einsum(
        "shqk,skhd->sqhd", probability, value_heads, preferred_element_type=jnp.float32
    )
    attended_low = attended.reshape(row_count, model_width).astype(jnp.bfloat16)
    branch = jnp.dot(attended_low, w_out, preferred_element_type=jnp.float32) + out_bias.astype(
        jnp.float32
    )
    middle = inputs + branch
    second_low = layer_norm(middle, mlp_gain, mlp_shift).astype(jnp.bfloat16)
    hidden = jnp.dot(second_low, w_up, preferred_element_type=jnp.float32) + up_bias.astype(
        jnp.float32
    )
    active_low = gelu_exact(hidden).astype(jnp.bfloat16)
    result = jnp.dot(active_low, w_down, preferred_element_type=jnp.float32) + down_bias.astype(
        jnp.float32
    )
    kept_column = kept_mask.reshape(row_count, 1)
    output_rows = (kept_column * (middle + result)).astype(jnp.bfloat16).reshape(block_shape)
    grad_result = kept_column * cotangent_rows.reshape(row_count, model_width).astype(jnp.float32)
    grad_low = grad_result.astype(jnp.bfloat16)
    grad_w_down = jnp.einsum("nf,nd->fd", active_low, grad_low, preferred_element_type=jnp.float32)
    grad_down_bias = jnp.sum(grad_low.astype(jnp.float32), axis=0)
    grad_active = jnp.einsum("nd,fd->nf", grad_low, w_down, preferred_element_type=jnp.float32)
    _, gelu_pull = jax.vjp(gelu_exact, hidden)
    grad_hidden = gelu_pull(grad_active)[0].astype(jnp.bfloat16)
    grad_w_up = jnp.einsum("nd,nf->df", second_low, grad_hidden, preferred_element_type=jnp.float32)
    grad_up_bias = jnp.sum(grad_hidden.astype(jnp.float32), axis=0)
    grad_second = jnp.einsum("nf,df->nd", grad_hidden, w_up, preferred_element_type=jnp.float32)
    _, second_pull = jax.vjp(layer_norm, middle, mlp_gain, mlp_shift)
    grad_mid_norm, grad_mlp_gain, grad_mlp_shift = second_pull(grad_second)
    grad_middle = grad_result + grad_mid_norm
    branch_low = grad_middle.astype(jnp.bfloat16)
    grad_w_out = jnp.einsum(
        "nd,ne->de", attended_low, branch_low, preferred_element_type=jnp.float32
    )
    grad_out_bias = jnp.sum(branch_low.astype(jnp.float32), axis=0)
    grad_attended = jnp.einsum(
        "ne,de->nd", branch_low, w_out, preferred_element_type=jnp.float32
    ).astype(jnp.bfloat16)
    key_back, value_back, code_back = (
        lax.all_gather(key_rows, "frame", axis=1, tiled=True),
        lax.all_gather(value_rows, "frame", axis=1, tiled=True),
        lax.all_gather(code_rows, "frame", axis=1, tiled=True),
    )
    scores, allowed = raw_scores(query_rows, key_back, segment_rows, code_back)
    value_heads = value_back.reshape(slot_count, key_length, HEADS, head_dim)
    key_heads = key_back.reshape(slot_count, key_length, HEADS, head_dim)
    scale = head_dim ** (-0.5)
    prob_back = jnp.where(allowed, jnp.exp(scores - log_total), 0.0)
    grad_heads = grad_attended.reshape(slot_count, length, HEADS, head_dim)
    query_heads = query_rows.reshape(slot_count, length, HEADS, head_dim)
    grad_prob = jnp.einsum(
        "sqhd,skhd->shqk", grad_heads, value_heads, preferred_element_type=jnp.float32
    )
    row_delta = jnp.sum(prob_back * grad_prob, axis=-1, keepdims=True)
    grad_scores = (prob_back * (grad_prob - row_delta)).astype(jnp.bfloat16)
    grad_query = (
        (
            jnp.einsum(
                "shqk,skhd->sqhd", grad_scores, key_heads, preferred_element_type=jnp.float32
            )
            * scale
        )
        .reshape(row_count, model_width)
        .astype(jnp.bfloat16)
    )
    grad_key_all = (
        jnp.einsum("shqk,sqhd->skhd", grad_scores, query_heads, preferred_element_type=jnp.float32)
        * scale
    ).reshape(slot_count, key_length, model_width)
    grad_value_all = jnp.einsum(
        "shqk,sqhd->skhd",
        prob_back.astype(jnp.bfloat16),
        grad_heads,
        preferred_element_type=jnp.float32,
    ).reshape(slot_count, key_length, model_width)
    grad_key, grad_value = (
        lax.psum_scatter(
            grad_key_all.astype(jnp.bfloat16), "frame", scatter_dimension=1, tiled=True
        ).astype(jnp.float32),
        lax.psum_scatter(
            grad_value_all.astype(jnp.bfloat16), "frame", scatter_dimension=1, tiled=True
        ).astype(jnp.float32),
    )
    grad_key_low = grad_key.reshape(row_count, model_width).astype(jnp.bfloat16)
    grad_value_low = grad_value.reshape(row_count, model_width).astype(jnp.bfloat16)
    grad_mixed = jnp.concatenate([grad_query, grad_key_low, grad_value_low], axis=1)
    grad_w_qkv = jnp.einsum("nd,ne->de", first_low, grad_mixed, preferred_element_type=jnp.float32)
    grad_query_bias = jnp.sum(grad_query.astype(jnp.float32), axis=0)
    grad_value_bias = jnp.sum(grad_value_low.astype(jnp.float32), axis=0)
    grad_first = jnp.einsum("ne,de->nd", grad_mixed, w_qkv, preferred_element_type=jnp.float32)
    _, first_pull = jax.vjp(layer_norm, inputs, attn_gain, attn_shift)
    grad_in_norm, grad_attn_gain, grad_attn_shift = first_pull(grad_first)
    input_rows = (grad_middle + grad_in_norm).reshape(block_shape)
    grads = (
        grad_attn_gain,
        grad_attn_shift,
        grad_w_qkv,
        grad_query_bias,
        grad_value_bias,
        grad_w_out,
        grad_out_bias,
        grad_mlp_gain,
        grad_mlp_shift,
        grad_w_up,
        grad_up_bias,
        grad_w_down,
        grad_down_bias,
    )
    return (output_rows, input_rows, grads)


def body(
    tokens,
    cotangent,
    frame_count,
    image_group,
    keep_mask,
    attn_norm_gain,
    attn_norm_bias,
    w_qkv,
    query_bias,
    value_bias,
    w_out,
    out_bias,
    mlp_norm_gain,
    mlp_norm_bias,
    w_up,
    up_bias,
    w_down,
    down_bias,
):
    frames_here = image_group.shape[1]
    block_width = keep_mask.shape[1] // frames_here
    frame_index = lax.axis_index("frame") * frames_here + jnp.arange(frames_here, dtype=jnp.int32)
    segment = jnp.where(frame_index[None, :] < frame_count[:, None], 0, 1 + image_group)
    token_segment = jnp.repeat(segment, block_width, axis=1)
    key_code = jnp.where(keep_mask == 1, token_segment, -1)
    kept_rows = keep_mask.astype(jnp.float32)
    output_list = []
    input_list = []
    totals = None
    for batch_index in range(MICRO):
        lower = batch_index * SLOT_MB
        upper = lower + SLOT_MB
        full = (
            lax.all_gather(attn_norm_gain, ("frame", "clip"), axis=0, tiled=True),
            lax.all_gather(attn_norm_bias, ("frame", "clip"), axis=0, tiled=True),
            lax.all_gather(w_qkv, ("frame", "clip"), axis=0, tiled=True),
            lax.all_gather(query_bias, ("frame", "clip"), axis=0, tiled=True),
            lax.all_gather(value_bias, ("frame", "clip"), axis=0, tiled=True),
            lax.all_gather(w_out, ("frame", "clip"), axis=0, tiled=True),
            lax.all_gather(out_bias, ("frame", "clip"), axis=0, tiled=True),
            lax.all_gather(mlp_norm_gain, ("frame", "clip"), axis=0, tiled=True),
            lax.all_gather(mlp_norm_bias, ("frame", "clip"), axis=0, tiled=True),
            lax.all_gather(w_up, ("frame", "clip"), axis=0, tiled=True),
            lax.all_gather(up_bias, ("frame", "clip"), axis=0, tiled=True),
            lax.all_gather(w_down, ("frame", "clip"), axis=0, tiled=True),
            lax.all_gather(down_bias, ("frame", "clip"), axis=0, tiled=True),
        )
        output_rows, input_rows, grads = layer_step(
            full,
            tokens[lower:upper],
            cotangent[lower:upper],
            token_segment[lower:upper],
            key_code[lower:upper],
            kept_rows[lower:upper],
        )
        output_list.append(output_rows)
        input_list.append(input_rows)
        shares = (
            lax.psum_scatter(grads[0], ("frame", "clip"), scatter_dimension=0, tiled=True),
            lax.psum_scatter(grads[1], ("frame", "clip"), scatter_dimension=0, tiled=True),
            lax.psum_scatter(grads[2], ("frame", "clip"), scatter_dimension=0, tiled=True),
            lax.psum_scatter(grads[3], ("frame", "clip"), scatter_dimension=0, tiled=True),
            lax.psum_scatter(grads[4], ("frame", "clip"), scatter_dimension=0, tiled=True),
            lax.psum_scatter(grads[5], ("frame", "clip"), scatter_dimension=0, tiled=True),
            lax.psum_scatter(grads[6], ("frame", "clip"), scatter_dimension=0, tiled=True),
            lax.psum_scatter(grads[7], ("frame", "clip"), scatter_dimension=0, tiled=True),
            lax.psum_scatter(grads[8], ("frame", "clip"), scatter_dimension=0, tiled=True),
            lax.psum_scatter(grads[9], ("frame", "clip"), scatter_dimension=0, tiled=True),
            lax.psum_scatter(grads[10], ("frame", "clip"), scatter_dimension=0, tiled=True),
            lax.psum_scatter(grads[11], ("frame", "clip"), scatter_dimension=0, tiled=True),
            lax.psum_scatter(grads[12], ("frame", "clip"), scatter_dimension=0, tiled=True),
        )
        totals = shares if totals is None else jax.tree.map(jnp.add, totals, shares)
    output = jnp.concatenate(output_list, axis=0)
    input_grad = jnp.concatenate(input_list, axis=0)
    return (
        output,
        input_grad,
        totals[0],
        totals[1],
        totals[2],
        totals[3],
        totals[4],
        totals[5],
        totals[6],
        totals[7],
        totals[8],
        totals[9],
        totals[10],
        totals[11],
        totals[12],
    )


def solution(mesh):
    placed = (
        P("clip", "frame", None),
        P("clip", "frame", None),
        P("clip"),
        P("clip", "frame"),
        P("clip", "frame"),
        P(("frame", "clip")),
        P(("frame", "clip")),
        P(("frame", "clip"), None),
        P(("frame", "clip")),
        P(("frame", "clip")),
        P(("frame", "clip"), None),
        P(("frame", "clip")),
        P(("frame", "clip")),
        P(("frame", "clip")),
        P(("frame", "clip"), None),
        P(("frame", "clip")),
        P(("frame", "clip"), None),
        P(("frame", "clip")),
    )
    return jax.shard_map(
        body,
        mesh=mesh,
        in_specs=placed,
        out_specs=(
            P("clip", "frame", None),
            P("clip", "frame", None),
            P(("frame", "clip")),
            P(("frame", "clip")),
            P(("frame", "clip"), None),
            P(("frame", "clip")),
            P(("frame", "clip")),
            P(("frame", "clip"), None),
            P(("frame", "clip")),
            P(("frame", "clip")),
            P(("frame", "clip")),
            P(("frame", "clip"), None),
            P(("frame", "clip")),
            P(("frame", "clip"), None),
            P(("frame", "clip")),
        ),
        check_vma=False,
    )
```

profile of v0, /device:TPU:0, one launch (start us, length us, event | category | flops | bytes accessed | tf_op | source)
XLA Modules:
  0.0 1151.0 jit_solution(13188558341055521618)
XLA Ops:
  15.5 42.7 %all-reduce.19 = (bf16[768]{0:T(1024)(128)(2,1)S(1)}, bf16[768]{0:T(1024)(128)(2,1)S(1)}, bf16[768]{0:T(1024)(128)(2,1)S(1)}, bf16[768]{0:T(1024)(128)(2,1)S(1)}...) all-reduce(bf16[768]{0:T(1024)(128)(2,1)S(1)} %dynamic-update-slice, ...), channel_id=1, replica_groups=mesh['frame'=4,'clip'=8] {'frame','clip'}, use_global_device_ids=true, to_apply=%add.1 | all-reduce | flops 9216 | bytes 36864
  65.7 8.2 all-gather.14.cloned.1.call-done
  99.3 5.2 all-gather
  104.5 5.4 all-gather.2
  132.7 5.1 fusion.60
  141.1 39.9 %all-gather.20.cloned.1.call-done = bf16[768,768]{1,0:T(8,128)(2,1)} async-done(((bf16[24,768]{1,0:T(8,128)(2,1)}), bf16[768,768]{1,0:T(8,128)(2,1)}) %all-gather.20.cloned.1.call-update) | async-done | bytes 1179664 | tf_op jit(solution)/shard_map/all_gather | solution.py:240
  184.8 18.4 %all-gather.32.cloned.1.call-done = bf16[4,320,768]{2,1,0:T(8,128)(2,1)} async-done(((bf16[4,80,768]{2,1,0:T(8,128)(2,1)}), bf16[4,320,768]{2,1,0:T(8,128)(2,1)}) %all-gather.32.cloned.1.call-update) | async-done | bytes 1966096 | tf_op jit(solution)/shard_map/all_gather | solution.py:76
  212.5 14.0 %all-gather.30.cloned.1.call-done = bf16[4,320,768]{2,1,0:T(8,128)(2,1)} async-done(((bf16[4,80,768]{2,1,0:T(8,128)(2,1)}), bf16[4,320,768]{2,1,0:T(8,128)(2,1)}) %all-gather.30.cloned.1.call-update) | async-done | bytes 1966096 | tf_op jit(solution)/shard_map/all_gather | solution.py:77
  239.3 53.8 %all-gather.22.cloned.1.call-done = bf16[768,3072]{1,0:T(8,128)(2,1)} async-done(((bf16[24,3072]{1,0:T(8,128)(2,1)}), bf16[768,3072]{1,0:T(8,128)(2,1)}) %all-gather.22.cloned.1.call-update) | async-done | bytes 4718608 | tf_op jit(solution)/shard_map/all_gather | solution.py:244
  293.1 6.2 convolution_add_fusion.2
  303.1 55.4 %all-gather.24.cloned.1.call-done = bf16[3072,768]{1,0:T(8,128)(2,1)} async-done(((bf16[96,768]{1,0:T(8,128)(2,1)}), bf16[3072,768]{1,0:T(8,128)(2,1)}) %all-gather.24.cloned.1.call-update) | async-done | bytes 4718608 | tf_op jit(solution)/shard_map/all_gather | solution.py:246
  358.6 13.9 %convert_reduce_fusion = (f32[3072]{0:T(1024)}, bf16[320,3072]{1,0:T(8,128)(2,1)S(1)}, f32[320,3072]{1,0:T(8,128)}) fusion(f32[320,3072]{1,0:T(8,128)} %convolution_add_fusion, bf16[320,768]{1,0:T(8,128)(2,1)S(1)} %copy-done.85, bf16[3072,768]{1,0:T(8,128)(2,1)} %all-gather.24.cloned.1.call-done), kind=kOutput, calls=%fused_computation.36 | convolution fusion | flops 1582691328 | bytes 15052800 | tf_op jit(solution)/shard_map/nd,fd->nf/dot_general | solution.py:111
  378.3 12.6 %convert_reduce_fusion.2 = (f32[3072]{0:T(1024)}, bf16[320,3072]{1,0:T(8,128)(2,1)S(1)}, f32[320,3072]{1,0:T(8,128)}) fusion(f32[320,3072]{1,0:T(8,128)S(1)} %copy-done.62, bf16[320,768]{1,0:T(8,128)(2,1)S(1)} %copy-done.102, bf16[3072,768]{1,0:T(8,128)(2,1)S(1)} %copy-done.203), kind=kOutput, calls=%fused_computation.38 | convolution fusion | flops 1582691328 | bytes 15052800 | tf_op jit(solution)/shard_map/nd,fd->nf/dot_general | solution.py:111
  418.7 5.2 all-gather.1
  428.2 6.7 multiply_reduce_fusion
  454.9 6.1 fusion.61
  470.1 6.5 multiply_reduce_fusion.2
  498.0 15.0 %convert_reduce_fusion.1 = (f32[3072]{0:T(1024)}, bf16[320,3072]{1,0:T(8,128)(2,1)S(1)}, f32[320,3072]{1,0:T(8,128)}) fusion(f32[320,3072]{1,0:T(8,128)S(1)} %convolution_add_fusion.1, bf16[320,768]{1,0:T(8,128)(2,1)S(1)} %copy-done.96, bf16[3072,768]{1,0:T(8,128)(2,1)} %all-gather.24.cloned.1.call-done), kind=kOutput, calls=%fused_computation.37 | convolution fusion | flops 1582691328 | bytes 15052800 | tf_op jit(solution)/shard_map/nd,fd->nf/dot_general | solution.py:111
  521.4 15.6 %reduce-scatter.11.cloned.1.call-done = bf16[4,80,768]{2,1,0:T(8,128)(2,1)} async-done(((bf16[4,320,768]{2,1,0:T(8,128)(2,1)}), bf16[4,80,768]{2,1,0:T(8,128)(2,1)}) %reduce-scatter.11.cloned.1.call-update) | async-done | bytes 491536 | tf_op jit(solution)/shard_map/reduce_scatter | solution.py:166
  556.8 5.4 fusion.48
  566.6 4.9 multiply_reduce_fusion.1
  588.5 4.9 fusion.114
  596.3 8.8 add_add_fusion.1
  621.5 5.1 add_add_fusion
  631.0 6.6 fusion.84
  644.4 5.0 add_add_fusion.2
  651.2 4.9 fusion.69
  667.8 5.4 multiply_reduce_fusion.7
  673.2 41.5 %all-reduce.18 = (f32[768]{0:T(1024)}, f32[768]{0:T(1024)}, f32[768]{0:T(1024)}, f32[768]{0:T(1024)}, f32[768]{0:T(1024)S(1)}, /*index=5*/f32[768]{0:T(1024)S(1)...) all-reduce(f32[768]{0:T(1024)S(1)} %add_add_fusion.24, ...), channel_id=34, replica_groups=mesh['frame'=4,'clip'=8] {'frame','clip'}, use_global_device_ids=true, to_apply=%region_40.41.clone | all-reduce | flops 9216 | bytes 73728
  735.5 142.0 %reduce-scatter.27.cloned.1.call-done = f32[24,3072]{1,0:T(8,128)} async-done(((f32[768,3072]{1,0:T(8,128)}), f32[24,3072]{1,0:T(8,128)}) %reduce-scatter.27.cloned.1.call-update) | async-done | bytes 294928 | tf_op jit(solution)/shard_map/reduce_scatter | solution.py:269
  877.5 141.1 %reduce-scatter.29.cloned.1.call-done = f32[96,768]{1,0:T(8,128)} async-done(((f32[3072,768]{1,0:T(8,128)}), f32[96,768]{1,0:T(8,128)}) %reduce-scatter.29.cloned.1.call-update) | async-done | bytes 294928 | tf_op jit(solution)/shard_map/reduce_scatter | solution.py:271
  1018.6 125.1 %reduce-scatter.23.cloned.1.call-done = f32[24,2304]{1,0:T(8,128)} async-done(((f32[768,2304]{1,0:T(8,128)}), f32[24,2304]{1,0:T(8,128)}) %reduce-scatter.23.cloned.1.call-update) | async-done | bytes 221200 | tf_op jit(solution)/shard_map/reduce_scatter | solution.py:262
  (716 shorter events, 296.6 us)
Async XLA Ops:
  7.2 66.7 %all-gather.14.cloned.1.call-start = ((), (), s32[]{:S(2)}) async-start(), calls=%async_computation.10 | async-start | bytes 3649536 | tf_op jit(solution)/shard_map/all_gather | solution.py:237
  7.9 110.8 %all-gather.18.cloned.1.call-start = ((), (), s32[]{:S(2)}) async-start(), calls=%async_computation.12 | async-start | bytes 2457600 | tf_op jit(solution)/shard_map/all_gather | solution.py:76
  63.8 117.3 %copy-start.17 = (f32[4,80,768]{2,1,0:T(8,128)}, f32[4,80,768]{2,1,0:T(8,128)S(1)}, u32[]{:S(2)}) copy-start(f32[4,80,768]{2,1,0:T(8,128)S(1)} %get-tuple-element.95) | copy-start | bytes 2949124
  79.8 50.0 %all-gather.16.cloned.1.call-start = ((), (), s32[]{:S(2)}) async-start(), calls=%async_computation.11 | async-start | bytes 2457600 | tf_op jit(solution)/shard_map/all_gather | solution.py:77
  88.8 92.2 %all-gather.20.cloned.1.call-start = ((), (), s32[]{:S(2)}) async-start(), calls=%async_computation.13 | async-start | bytes 1216512 | tf_op jit(solution)/shard_map/all_gather | solution.py:240
  89.4 113.8 %all-gather.32.cloned.1.call-start = ((), (), s32[]{:S(2)}) async-start(), calls=%async_computation.19 | async-start | bytes 2457600 | tf_op jit(solution)/shard_map/all_gather | solution.py:76
  91.6 135.0 %all-gather.30.cloned.1.call-start = ((), (), s32[]{:S(2)}) async-start(), calls=%async_computation.18 | async-start | bytes 2457600 | tf_op jit(solution)/shard_map/all_gather | solution.py:77
  92.1 201.0 %all-gather.22.cloned.1.call-start = ((), (), s32[]{:S(2)}) async-start(), calls=%async_computation.14 | async-start | bytes 4866048 | tf_op jit(solution)/shard_map/all_gather | solution.py:244
  92.9 265.7 %all-gather.24.cloned.1.call-start = ((), (), s32[]{:S(2)}) async-start(), calls=%async_computation.15 | async-start | bytes 4866048 | tf_op jit(solution)/shard_map/all_gather | solution.py:246
  93.6 347.4 %all-gather.28.cloned.1.call-start = ((), (), s32[]{:S(2)}) async-start(), calls=%async_computation.17 | async-start | bytes 2457600 | tf_op jit(solution)/shard_map/all_gather | solution.py:76
  95.8 354.6 %all-gather.26.cloned.1.call-start = ((), (), s32[]{:S(2)}) async-start(), calls=%async_computation.16 | async-start | bytes 2457600 | tf_op jit(solution)/shard_map/all_gather | solution.py:77
  97.2 202.2 %copy-start.104 = (f32[768]{0:T(1024)}, f32[768]{0:T(1024)S(1)}, u32[]{:S(2)}) copy-start(f32[768]{0:T(1024)S(1)} %convert_element_type.455) | copy-start | bytes 9220
  97.2 139.6 %copy-start.124 = (f32[768]{0:T(1024)}, f32[768]{0:T(1024)S(1)}, u32[]{:S(2)}) copy-start(f32[768]{0:T(1024)S(1)} %convert_element_type.453) | copy-start | bytes 9220
  118.7 398.3 %reduce-scatter.13.cloned.1.call-start = ((), (), s32[]{:S(2)}) async-start(), calls=%async_computation.21 | async-start | bytes 2457600 | tf_op jit(solution)/shard_map/reduce_scatter | solution.py:169
  183.1 210.6 %copy-start.120 = (f32[320]{0:T(512)}, f32[320]{0:T(512)S(1)}, u32[]{:S(2)}) copy-start(f32[320]{0:T(512)S(1)} %broadcast_multiply_fusion.2) | copy-start | bytes 3844
  235.6 57.5 %copy-start.23 = (f32[320,768]{1,0:T(8,128)S(1)}, f32[320,768]{1,0:T(8,128)}, u32[]{:S(2)}) copy-start(f32[320,768]{1,0:T(8,128)} %copy-done.22) | copy-start | bytes 2949124
  236.8 62.5 %copy-start.51 = (bf16[320,768]{0,1:T(8,128)(2,1)}, bf16[320,768]{0,1:T(8,128)(2,1)S(1)}, u32[]{:S(2)}) copy-start(bf16[320,768]{0,1:T(8,128)(2,1)S(1)} %convert_element_type.483) | copy-start | bytes 1474564
  239.0 154.7 %copy-start.26 = (f32[320,768]{1,0:T(8,128)}, f32[320,768]{1,0:T(8,128)S(1)}, u32[]{:S(2)}) copy-start(f32[320,768]{1,0:T(8,128)S(1)} %get-tuple-element.129) | copy-start | bytes 2949124
  239.0 154.6 %copy-start.129 = (f32[320]{0:T(512)}, f32[320]{0:T(512)S(1)}, u32[]{:S(2)}) copy-start(f32[320]{0:T(512)S(1)} %broadcast_multiply_fusion) | copy-start | bytes 3844
  239.3 60.0 %copy-start.165 = (f32[320]{0:T(512)}, f32[320]{0:T(512)S(1)}, u32[]{:S(2)}) copy-start(f32[320]{0:T(512)S(1)} %multiply_reduce_fusion.15) | copy-start | bytes 3844
  239.3 154.4 %copy-start.155 = (f32[320]{0:T(512)}, f32[320]{0:T(512)S(1)}, u32[]{:S(2)}) copy-start(f32[320]{0:T(512)S(1)} %fusion.91) | copy-start | bytes 3844
  239.3 60.0 %copy-start.182 = (f32[3072]{0:T(1024)S(1)}, f32[3072]{0:T(1024)}, u32[]{:S(2)}) copy-start(f32[3072]{0:T(1024)} %convert_element_type.457) | copy-start | bytes 36868
  299.4 59.2 %copy-start.85 = (bf16[320,768]{1,0:T(8,128)(2,1)S(1)}, bf16[320,768]{1,0:T(8,128)(2,1)}, u32[]{:S(2)}) copy-start(bf16[320,768]{1,0:T(8,128)(2,1)} %get-tuple-element.94) | copy-start | bytes 1474564
  407.7 110.6 %reduce-scatter.21.cloned.1.call-start = ((), (), s32[]{:S(2)}) async-start(), calls=%async_computation.25 | async-start | bytes 2457600 | tf_op jit(solution)/shard_map/reduce_scatter | solution.py:169
  418.4 101.5 %reduce-scatter.19.cloned.1.call-start = ((), (), s32[]{:S(2)}) async-start(), calls=%async_computation.24 | async-start | bytes 2457600 | tf_op jit(solution)/shard_map/reduce_scatter | solution.py:166
  450.3 86.8 %reduce-scatter.11.cloned.1.call-start = ((), (), s32[]{:S(2)}) async-start(), calls=%async_computation.20 | async-start | bytes 2457600 | tf_op jit(solution)/shard_map/reduce_scatter | solution.py:166
  493.6 143.9 %reduce-scatter.17.cloned.1.call-start = ((), (), s32[]{:S(2)}) async-start(), calls=%async_computation.23 | async-start | bytes 2457600 | tf_op jit(solution)/shard_map/reduce_scatter | solution.py:169
  566.5 72.4 %reduce-scatter.15.cloned.1.call-start = ((), (), s32[]{:S(2)}) async-start(), calls=%async_computation.22 | async-start | bytes 2457600 | tf_op jit(solution)/shard_map/reduce_scatter | solution.py:166
  582.0 153.5 %reduce-scatter.25.cloned.1.call-start = ((), (), s32[]{:S(2)}) async-start(), calls=%async_computation.27 | async-start | bytes 2433024 | tf_op jit(solution)/shard_map/reduce_scatter | solution.py:265
  588.4 289.1 %reduce-scatter.27.cloned.1.call-start = ((), (), s32[]{:S(2)}) async-start(), calls=%async_computation.28 | async-start | bytes 9732096 | tf_op jit(solution)/shard_map/reduce_scatter | solution.py:269
  605.1 413.5 %reduce-scatter.29.cloned.1.call-start = ((), (), s32[]{:S(2)}) async-start(), calls=%async_computation.29 | async-start | bytes 9732096 | tf_op jit(solution)/shard_map/reduce_scatter | solution.py:271
  626.6 517.2 %reduce-scatter.23.cloned.1.call-start = ((), (), s32[]{:S(2)}) async-start(), calls=%async_computation.26 | async-start | bytes 7299072 | tf_op jit(solution)/shard_map/reduce_scatter | solution.py:262
  (205 other events, 1552.6 us)
Sparse Core Ops, SparseCore 0:
  10.9 62.9 all-gather.13
  79.9 20.6 all-gather.17
  102.1 21.8 all-gather.15
  126.8 54.1 all-gather.19
  182.4 20.7 all-gather.31
  204.6 21.8 all-gather.29
  229.4 63.6 all-gather.21
  296.0 62.4 all-gather.23
  360.1 20.6 all-gather.27
  382.2 21.8 all-gather.25
  407.9 29.4 reduce-scatter.12
  439.9 30.6 reduce-scatter.20
  473.2 30.6 reduce-scatter.18
  506.4 30.6 reduce-scatter.10
  566.7 30.6 reduce-scatter.16
  599.9 30.6 reduce-scatter.14
  636.3 99.1 reduce-scatter.24
  742.8 134.6 reduce-scatter.26
  884.0 134.5 reduce-scatter.28
  1025.7 118.0 reduce-scatter.22
where the time goes:
time: 1160 us; the launch traced here: 1150 us
  waiting for transfers between devices  622 us (54%)
  matrix products  224 us (19%)
  local copies, waits for them, and re-layouts  130 us (11%)
  blocking collectives  99.9 us (9%)
  other arithmetic  55.7 us (5%)
  between operations  18 us (2%)
    reduce_scatter x1, waiting for transfers between devices, body(): lax.psum_scatter(grads[9], ('frame', 'clip'), scatter_dimension=0, tiled=...  142 us
    reduce_scatter x1, waiting for transfers between devices, body(): lax.psum_scatter(grads[11], ('frame', 'clip'), scatter_dimension=0, tiled...  141 us
    reduce_scatter x1, waiting for transfers between devices, body(): lax.psum_scatter(grads[2], ('frame', 'clip'), scatter_dimension=0, tiled=...  125 us
    unnamed x2, blocking collectives  84.3 us
    all_gather x1, waiting for transfers between devices, body(): lax.all_gather(w_down, ('frame', 'clip'), axis=0, tiled=True)  55.4 us
    all_gather x1, waiting for transfers between devices, body(): lax.all_gather(w_up, ('frame', 'clip'), axis=0, tiled=True)  53.8 us
    unnamed x465, local copies, waits for them, and re-layouts  44.2 us
    dot_general x3, matrix products, layer_step(): jnp.einsum('nd,fd->nf', grad_low, w_down, preferred_element_type=jnp.floa...  41.6 us
  transfers between devices with their start and end apart: 20, of which 11 were waited for; matrix products, arithmetic and copies ran while one was open for 30% of the time, Pallas kernels for 0%

commit v1 on v0

--- a/solution.py
+++ b/solution.py
@@ -4,11 +4,101 @@
 from jax.sharding import PartitionSpec as P
 
 HEADS = 12
-SLOT_MB = 4
-MICRO = 3
-
-
 EPSILON = 1e-06
+AXES = ("frame", "clip")
+
+
+class Grid:
+    def __init__(self, frames, clips):
+        self.frames = frames
+        self.clips = clips
+        self.sizes = {"x": frames // 2, "core": 2, "z": clips // 2, "y": 2}
+
+    def here(self):
+        frame = lax.axis_index("frame")
+        clip = lax.axis_index("clip")
+        return {"x": frame // 2, "core": frame % 2, "z": clip // 2, "y": clip % 2}
+
+    def swap(self, value, **flips):
+        pairs = []
+        for index in range(self.frames * self.clips):
+            frame, clip = divmod(index, self.clips)
+            at = {"x": frame // 2, "core": frame % 2, "z": clip // 2, "y": clip % 2}
+            for name, bits in flips.items():
+                at[name] ^= bits
+            other = (at["x"] * 2 + at["core"]) * self.clips + at["z"] * 2 + at["y"]
+            pairs.append((index, other))
+        return lax.ppermute(value, AXES, pairs)
+
+
+def put(buffer, piece, axis, index):
+    return lax.dynamic_update_index_in_dim(buffer, piece, index, axis)
+
+
+def pick(value, axis, index):
+    return lax.dynamic_index_in_dim(value, index, axis, keepdims=False)
+
+
+def gather_axis(grid, here, value, name, axis):
+    count = grid.sizes[name]
+    parts = [value] + [grid.swap(value, **{name: bits}) for bits in range(1, count)]
+    shape = value.shape[:axis] + (count,) + value.shape[axis:]
+    buffer = jnp.zeros(shape, value.dtype)
+    for bits, part in enumerate(parts):
+        buffer = put(buffer, part, axis, here[name] ^ bits)
+    return buffer
+
+
+def gather_weight(grid, here, shard, order):
+    have = []
+    value = shard
+    for name in order:
+        axis = sum(1 for done in have if "x core z y".split().index(done) < "x core z y".split().index(name))
+        value = gather_axis(grid, here, value, name, axis)
+        have.append(name)
+    return value.reshape((-1,) + shard.shape[1:])
+
+
+def scatter_weight(grid, here, grad, order, keep=jnp.bfloat16):
+    sizes = grid.sizes
+    rows = grad.shape[0] // (grid.frames * grid.clips)
+    value = grad.reshape((sizes["x"], sizes["core"], sizes["z"], sizes["y"], rows) + grad.shape[1:])
+    left = ["x", "core", "z", "y"]
+    for step, name in enumerate(order):
+        axis = left.index(name)
+        total = pick(value, axis, here[name]).astype(jnp.float32)
+        for bits in range(1, sizes[name]):
+            sent = pick(value, axis, here[name] ^ bits)
+            total = total + grid.swap(sent, **{name: bits}).astype(jnp.float32)
+        left.remove(name)
+        value = total if step == len(order) - 1 else total.astype(keep)
+    return value
+
+
+def to_slots(grid, here, value):
+    own = value.shape[0] // grid.frames
+    frame = here["x"] * 2 + here["core"]
+    pieces = []
+    for bits in range(grid.frames):
+        piece = lax.dynamic_slice_in_dim(value, (frame ^ bits) * own, own, 0)
+        if bits:
+            piece = grid.swap(piece, x=bits // 2, core=bits % 2)
+        pieces.append(piece)
+    return jnp.concatenate(pieces, axis=1)
+
+
+def from_slots(grid, here, value):
+    frames = grid.frames
+    own, length = value.shape[:2]
+    width = length // frames
+    frame = here["x"] * 2 + here["core"]
+    buffer = jnp.zeros((own * frames, width) + value.shape[2:], value.dtype)
+    for bits in range(frames):
+        piece = value[:, bits * width : (bits + 1) * width]
+        if bits:
+            piece = grid.swap(piece, x=bits // 2, core=bits % 2)
+        buffer = lax.dynamic_update_slice_in_dim(buffer, piece, (frame ^ bits) * own, 0)
+    return buffer
 
 
 def layer_norm(values, gain, shift):
@@ -72,11 +162,7 @@
         .astype(jnp.bfloat16)
         .reshape(block_shape)
     )
-    key_all, value_all, code_all = (
-        lax.all_gather(key_rows, "frame", axis=1, tiled=True),
-        lax.all_gather(value_rows, "frame", axis=1, tiled=True),
-        lax.all_gather(code_rows, "frame", axis=1, tiled=True),
-    )
+    key_all, value_all, code_all = (key_rows, value_rows, code_rows)
     key_length = key_all.shape[1]
     scores, allowed = raw_scores(query_rows, key_all, segment_rows, code_all)
     masked = jnp.where(allowed, scores, -1e30)
@@ -125,11 +211,7 @@
     grad_attended = jnp.einsum(
         "ne,de->nd", branch_low, w_out, preferred_element_type=jnp.float32
     ).astype(jnp.bfloat16)
-    key_back, value_back, code_back = (
-        lax.all_gather(key_rows, "frame", axis=1, tiled=True),
-        lax.all_gather(value_rows, "frame", axis=1, tiled=True),
-        lax.all_gather(code_rows, "frame", axis=1, tiled=True),
-    )
+    key_back, value_back, code_back = (key_rows, value_rows, code_rows)
     scores, allowed = raw_scores(query_rows, key_back, segment_rows, code_back)
     value_heads = value_back.reshape(slot_count, key_length, HEADS, head_dim)
     key_heads = key_back.reshape(slot_count, key_length, HEADS, head_dim)
@@ -162,14 +244,7 @@
         grad_heads,
         preferred_element_type=jnp.float32,
     ).reshape(slot_count, key_length, model_width)
-    grad_key, grad_value = (
-        lax.psum_scatter(
-            grad_key_all.astype(jnp.bfloat16), "frame", scatter_dimension=1, tiled=True
-        ).astype(jnp.float32),
-        lax.psum_scatter(
-            grad_value_all.astype(jnp.bfloat16), "frame", scatter_dimension=1, tiled=True
-        ).astype(jnp.float32),
-    )
+    grad_key, grad_value = (grad_key_all, grad_value_all)
     grad_key_low = grad_key.reshape(row_count, model_width).astype(jnp.bfloat16)
     grad_value_low = grad_value.reshape(row_count, model_width).astype(jnp.bfloat16)
     grad_mixed = jnp.concatenate([grad_query, grad_key_low, grad_value_low], axis=1)
@@ -199,6 +274,7 @@
 
 
 def body(
+    grid,
     tokens,
     cotangent,
     frame_count,
@@ -218,82 +294,84 @@
     w_down,
     down_bias,
 ):
+    here = grid.here()
     frames_here = image_group.shape[1]
     block_width = keep_mask.shape[1] // frames_here
     frame_index = lax.axis_index("frame") * frames_here + jnp.arange(frames_here, dtype=jnp.int32)
     segment = jnp.where(frame_index[None, :] < frame_count[:, None], 0, 1 + image_group)
     token_segment = jnp.repeat(segment, block_width, axis=1)
-    key_code = jnp.where(keep_mask == 1, token_segment, -1)
-    kept_rows = keep_mask.astype(jnp.float32)
-    output_list = []
-    input_list = []
-    totals = None
-    for batch_index in range(MICRO):
-        lower = batch_index * SLOT_MB
-        upper = lower + SLOT_MB
-        full = (
-            lax.all_gather(attn_norm_gain, ("frame", "clip"), axis=0, tiled=True),
-            lax.all_gather(attn_norm_bias, ("frame", "clip"), axis=0, tiled=True),
-            lax.all_gather(w_qkv, ("frame", "clip"), axis=0, tiled=True),
-            lax.all_gather(query_bias, ("frame", "clip"), axis=0, tiled=True),
-            lax.all_gather(value_bias, ("frame", "clip"), axis=0, tiled=True),
-            lax.all_gather(w_out, ("frame", "clip"), axis=0, tiled=True),
-            lax.all_gather(out_bias, ("frame", "clip"), axis=0, tiled=True),
-            lax.all_gather(mlp_norm_gain, ("frame", "clip"), axis=0, tiled=True),
-            lax.all_gather(mlp_norm_bias, ("frame", "clip"), axis=0, tiled=True),
-            lax.all_gather(w_up, ("frame", "clip"), axis=0, tiled=True),
-            lax.all_gather(up_bias, ("frame", "clip"), axis=0, tiled=True),
-            lax.all_gather(w_down, ("frame", "clip"), axis=0, tiled=True),
-            lax.all_gather(down_bias, ("frame", "clip"), axis=0, tiled=True),
-        )
-        output_rows, input_rows, grads = layer_step(
-            full,
-            tokens[lower:upper],
-            cotangent[lower:upper],
-            token_segment[lower:upper],
-            key_code[lower:upper],
-            kept_rows[lower:upper],
-        )
-        output_list.append(output_rows)
-        input_list.append(input_rows)
-        shares = (
-            lax.psum_scatter(grads[0], ("frame", "clip"), scatter_dimension=0, tiled=True),
-            lax.psum_scatter(grads[1], ("frame", "clip"), scatter_dimension=0, tiled=True),
-            lax.psum_scatter(grads[2], ("frame", "clip"), scatter_dimension=0, tiled=True),
-            lax.psum_scatter(grads[3], ("frame", "clip"), scatter_dimension=0, tiled=True),
-            lax.psum_scatter(grads[4], ("frame", "clip"), scatter_dimension=0, tiled=True),
-            lax.psum_scatter(grads[5], ("frame", "clip"), scatter_dimension=0, tiled=True),
-            lax.psum_scatter(grads[6], ("frame", "clip"), scatter_dimension=0, tiled=True),
-            lax.psum_scatter(grads[7], ("frame", "clip"), scatter_dimension=0, tiled=True),
-            lax.psum_scatter(grads[8], ("frame", "clip"), scatter_dimension=0, tiled=True),
-            lax.psum_scatter(grads[9], ("frame", "clip"), scatter_dimension=0, tiled=True),
-            lax.psum_scatter(grads[10], ("frame", "clip"), scatter_dimension=0, tiled=True),
-            lax.psum_scatter(grads[11], ("frame", "clip"), scatter_dimension=0, tiled=True),
-            lax.psum_scatter(grads[12], ("frame", "clip"), scatter_dimension=0, tiled=True),
-        )
-        totals = shares if totals is None else jax.tree.map(jnp.add, totals, shares)
-    output = jnp.concatenate(output_list, axis=0)
-    input_grad = jnp.concatenate(input_list, axis=0)
+    tags = to_slots(grid, here, token_segment * 2 + keep_mask)
+    token_segment = tags // 2
+    keep_slots = tags % 2
+    key_code = jnp.where(keep_slots == 1, token_segment, -1)
+    kept_rows = keep_slots.astype(jnp.float32)
+
+    rows = w_out.shape[0]
+    ratio = up_bias.shape[0] // rows
+    small = jnp.stack(
+        [attn_norm_gain, attn_norm_bias, query_bias, value_bias, out_bias, mlp_norm_gain, mlp_norm_bias, down_bias],
+        axis=1,
+    )
+    small = jnp.concatenate([small, up_bias.reshape(rows, ratio)], axis=1)
+    small = jnp.pad(small, ((0, 0), (0, 128 - small.shape[1])))
+    token_rows = to_slots(grid, here, tokens)
+
+    def gathered(shard):
+        width = shard.shape[1]
+        half = (width // 256) * 128
+        left = gather_weight(grid, here, shard[:, :half], ("z", "x", "y", "core"))
+        right = gather_weight(grid, here, shard[:, half:], ("z", "y", "x", "core"))
+        return jnp.concatenate([left, right], axis=1)
+
+    mixed = gathered(jnp.concatenate([w_qkv, small], axis=1))
+    qkv_full = mixed[:, : w_qkv.shape[1]]
+    small_full = mixed[:, w_qkv.shape[1] :]
+    vectors = [small_full[:, i] for i in range(8)]
+    up_bias_full = small_full[:, 8 : 8 + ratio].reshape(-1)
+    out_full = gathered(w_out)
+    up_full = gathered(w_up)
+    cotangent_rows = to_slots(grid, here, cotangent)
+    down_full = gathered(w_down)
+    full = (
+        vectors[0], vectors[1], qkv_full, vectors[2], vectors[3], out_full, vectors[4],
+        vectors[5], vectors[6], up_full, up_bias_full, down_full, vectors[7],
+    )
+    output_rows, input_rows, grads = layer_step(
+        full, token_rows, cotangent_rows, token_segment, key_code, kept_rows
+    )
+    output = from_slots(grid, here, output_rows)
+    input_grad = from_slots(grid, here, input_rows.astype(jnp.bfloat16)).astype(jnp.float32)
+
+    def scattered(grad):
+        low = grad.astype(jnp.bfloat16)
+        half = (grad.shape[1] // 256) * 128
+        left = scatter_weight(grid, here, low[:, :half], ("core", "x", "y", "z"))
+        right = scatter_weight(grid, here, low[:, half:], ("core", "y", "x", "z"))
+        return jnp.concatenate([left, right], axis=1)
+
+    g_down = scattered(grads[11])
+    g_up = scattered(grads[9])
+    g_out = scattered(grads[5])
+    g_qkv = scattered(grads[2])
+    devices = grid.frames * grid.clips
+    order = (0, 1, 3, 4, 6, 7, 8, 12)
+    pack = jnp.concatenate(
+        [grads[i].reshape(devices, rows) for i in order] + [grads[10].reshape(devices, rows * ratio)], axis=1
+    )
+    pack = scatter_weight(grid, here, pack, ("core", "x", "y", "z"), jnp.float32)[0]
+    v = {g: pack[i * rows : (i + 1) * rows] for i, g in enumerate(order)}
     return (
-        output,
-        input_grad,
-        totals[0],
-        totals[1],
-        totals[2],
-        totals[3],
-        totals[4],
-        totals[5],
-        totals[6],
-        totals[7],
-        totals[8],
-        totals[9],
-        totals[10],
-        totals[11],
-        totals[12],
+        output, input_grad, v[0], v[1], g_qkv, v[3], v[4], g_out, v[6], v[7], v[8],
+        g_up, pack[8 * rows :], g_down, v[12],
     )
 
 
 def solution(mesh):
+    grid = Grid(mesh.shape["frame"], mesh.shape["clip"])
+
+    def run(*arguments):
+        return body(grid, *arguments)
+
     placed = (
         P("clip", "frame", None),
         P("clip", "frame", None),
@@ -315,7 +393,7 @@
         P(("frame", "clip")),
     )
     return jax.shard_map(
-        body,
+        run,
         mesh=mesh,
         in_specs=placed,
         out_specs=(

time: 1160 us -> 712 us (0.61)
  waiting for transfers between devices: 622 us -> 146 us
  starting transfers between devices: 1.2 us -> 141 us
  blocking collectives: 99.9 us -> 0 us
  local copies, waits for them, and re-layouts: 130 us -> 199 us
  matrix products: 224 us -> 158 us
  between operations: 18 us -> 3.6 us
    reduce_scatter x10 -> x0, waiting for transfers between devices: 429 us -> none  [the longest x1 142 us: body(): lax.psum_scatter(grads[9], ('frame', 'clip'), scatter_dimension=0, tiled=...]
    all_gather x10 -> x0, waiting for transfers between devices: 190 us -> none  [the longest x1 55.4 us: body(): lax.all_gather(w_down, ('frame', 'clip'), axis=0, tiled=True)]
    ppermute x0 -> x117, waiting for transfers between devices: none -> 146 us  [swap(): return lax.ppermute(value, AXES, pairs)]
    ppermute x0 -> x117, starting transfers between devices: none -> 141 us  [swap(): return lax.ppermute(value, AXES, pairs)]
    unnamed x2 -> x0, blocking collectives: 84.3 us -> none
    dynamic_update_slice x0 -> x85, local copies, waits for them, and re-layouts: none -> 53.4 us  [the longest x79 53.3 us: put(): return lax.dynamic_update_index_in_dim(buffer, piece, index, axis)]
    another operation x0 -> x32, local copies, waits for them, and re-layouts: none -> 51.2 us  [the longest x2 23.7 us: layer_step(): value_heads = value_all.reshape(slot_count, key_length, HEADS, head_dim)]
    unnamed x465 -> x214, local copies, waits for them, and re-layouts: 44.2 us -> 13 us
  transfers between devices with their start and end apart: 20 -> 117, of which waited for: 11 -> 44; matrix products, arithmetic and copies ran while one was open for 30% -> 37% of each run, Pallas kernels for 0% -> 0%
where the time goes in v1:
time: 712 us; the launch traced here: 701 us
  local copies, waits for them, and re-layouts  199 us (28%)
  matrix products  158 us (22%)
  waiting for transfers between devices  146 us (21%)
  starting transfers between devices  141 us (20%)
  other arithmetic  53.7 us (8%)
    ppermute x117, waiting for transfers between devices, swap(): return lax.ppermute(value, AXES, pairs)  146 us
    ppermute x117, starting transfers between devices, swap(): return lax.ppermute(value, AXES, pairs)  141 us
    dynamic_update_slice x79, local copies, waits for them, and re-layouts, put(): return lax.dynamic_update_index_in_dim(buffer, piece, index, axis)  53.3 us
    dot_general x1, matrix products, layer_step(): jnp.dot(second_low, w_up, preferred_element_type=jnp.float32)  35.8 us
    another operation x2, local copies, waits for them, and re-layouts, layer_step(): value_heads = value_all.reshape(slot_count, key_length, HEADS, head_dim)  23.7 us
    dot_general x1, matrix products, layer_step(): jnp.einsum('nd,fd->nf', grad_low, w_down, preferred_element_type=jnp.floa...  15.3 us
  transfers between devices with their start and end apart: 117, of which 44 were waited for; matrix products, arithmetic and copies ran while one was open for 37% of the time, Pallas kernels for 0%

profile of v1, /device:TPU:0, one launch (start us, length us, event | category | flops | bytes accessed | tf_op | source)
XLA Modules:
  0.0 701.0 jit_solution(12006836657357988769)
XLA Ops:
  87.4 8.8 %collective-permute-done.21 = bf16[4,24,384]{2,1,0:T(8,128)(2,1)S(1)} collective-permute-done((bf16[4,24,384]{2,1,0:T(8,128)(2,1)S(1)}, bf16[4,24,384]{2,1,0:T(8,128)(2,1)S(1)}, u32[]{:S(2)}, u32[]{:S(2)}) %collective-permute-start.21) | collective-permute-done | bytes 73760 | tf_op jit(solution)/shard_map/ppermute | solution.py:31
  160.3 5.4 collective-permute-done.59
  181.3 7.7 %collective-permute-done.40 = bf16[4,2,24,1536]{3,2,1,0:T(8,128)(2,1)} collective-permute-done((bf16[4,2,24,1536]{3,2,1,0:T(8,128)(2,1)}, bf16[4,2,24,1536]{3,2,1,0:T(8,128)(2,1)}, u32[]{:S(2)}, u32[]{:S(2)}) %collective-permute-start.40) | collective-permute-done | bytes 589856 | tf_op jit(solution)/shard_map/ppermute | solution.py:31
  191.0 9.8 %collective-permute-done.52 = bf16[4,2,96,384]{3,2,1,0:T(8,128)(2,1)S(1)} collective-permute-done((bf16[4,2,96,384]{3,2,1,0:T(8,128)(2,1)}, bf16[4,2,96,384]{3,2,1,0:T(8,128)(2,1)S(1)}, u32[]{:S(2)}, u32[]{:S(2)}) %collective-permute-start.52) | collective-permute-done | bytes 589856 | tf_op jit(solution)/shard_map/ppermute | solution.py:31
  225.4 5.6 reshape.784
  231.1 5.9 copy.88
  237.0 5.6 reshape.785
  242.6 5.9 copy.89
  248.5 5.6 reshape.783
  254.1 18.1 %copy.90 = bf16[3,320,12,64]{1,3,2,0:T(8,128)(2,1)} copy(bf16[3,320,12,64]{3,2,1,0:T(8,128)(2,1)} %reshape.783) | data formatting | bytes 2949120 | tf_op jit(solution)/shard_map/reshape;reshape | solution.py:174
  272.2 11.2 %select_reduce_fusion = (f32[3,12,320]{2,1,0:T(8,128)S(1)}, f32[3,12,320,320]{2,3,1,0:T(8,128)}) fusion(pred[3,320,320]{1,2,0:T(8,128)(4,1)S(1)} %broadcast_compare_fusion, bf16[3,320,12,64]{1,3,2,0:T(8,128)(2,1)} %copy.88, bf16[3,320,12,64]{1,3,2,0:T(8,128)(2,1)} %copy.89), kind=kOutput, calls=%fused_computation.6 | convolution fusion | flops 482906880 | bytes 18048000 | tf_op jit(solution)/shard_map/sqhd,skhd->shqk/dot_general | solution.py:120
  283.4 10.6 %fusion = f32[3,12,320]{2,1,0:T(8,128)S(1)} fusion(f32[3,12,320,320]{2,3,1,0:T(8,128)} %get-tuple-element.129, f32[3,12,320]{2,1,0:T(8,128)S(1)} %get-tuple-element.128, pred[3,320,320]{1,2,0:T(8,128)(4,1)S(1)} %broadcast_compare_fusion), kind=kLoop, calls=%fused_computation.7 | loop fusion | flops 18420480 | bytes 15144960 | tf_op jit(solution)/shard_map/reduce_sum | solution.py:171
  294.0 12.4 %convert_bitcast_fusion = bf16[3,320,12,64]{1,3,2,0:T(8,128)(2,1)S(1)} fusion(bf16[3,320,12,64]{1,3,2,0:T(8,128)(2,1)} %copy.90, f32[3,12,320,320]{2,3,1,0:T(8,128)} %get-tuple-element.129, f32[3,12,320]{2,1,0:T(8,128)S(1)} %fusion, f32[3,12,320]{2,1,0:T(8,128)S(1)} %get-tuple-element.128, pred[3,320,320]{1,2,0:T(8,128)(4,1)S(1)} %broadcast_compare_fusion), kind=kOutput, calls=%fused_computation.81 | convolution fusion | flops 494714880 | bytes 18094080 | tf_op jit(solution)/shard_map/shqk,skhd->sqhd/dot_general | solution.py:175
  309.4 5.4 convert_element_type.671
  325.7 35.8 %multiply_convert_fusion.1 = (bf16[960,3072]{1,0:T(8,128)(2,1)}, f32[960,3072]{1,0:T(8,128)}, f32[960,3072]{1,0:T(8,128)}) fusion(f32[3072]{0:T(1024)S(1)} %reshape.748, bf16[768,1536]{1,0:T(8,128)(2,1)S(1)} %bitcast.573, bf16[768,1536]{1,0:T(8,128)(2,1)S(1)} %bitcast.575, f32[960,768]{1,0:T(8,128)S(1)} %get-tuple-element.131, f32[768]{0:T(1024)S(1)} %copy-done.100, ...), kind=kOutput, calls=%fused_computation.11 | convolution fusion | flops 4737613824 | bytes 37185024 | tf_op jit(solution)/shard_map/dot_general | solution.py:184
  366.6 15.3 %convert_reduce_fusion = (f32[3072]{0:T(1024)S(1)}, bf16[960,3072]{1,0:T(8,128)(2,1)}) fusion(f32[960,3072]{1,0:T(8,128)} %get-tuple-element.36, bf16[960,768]{1,0:T(8,128)(2,1)S(1)} %copy-done.58, bf16[3072,384]{1,0:T(8,128)(2,1)S(1)} %bitcast.571, bf16[3072,384]{1,0:T(8,128)(2,1)} %bitcast.104, f32[960,3072]{1,0:T(8,128)} %get-tuple-element.132, ...), kind=kOutput, calls=%fused_computation.9 | convolution fusion | flops 4589417472 | bytes 35708928 | tf_op jit(solution)/shard_map/nd,fd->nf/dot_general | solution.py:197
  381.8 10.0 %convolution_convert_fusion.1 = bf16[768,3072]{1,0:T(8,128)(2,1)} fusion(bf16[960,3072]{1,0:T(8,128)(2,1)} %get-tuple-element.142, f32[960,768]{1,0:T(8,128)S(1)} %get-tuple-element.131, f32[768]{0:T(1024)S(1)} %copy-done.100, f32[768]{0:T(1024)S(1)} %get-tuple-element.23, f32[960]{0:T(1024)S(1)} %fusion.88, f32[960]{0:T(1024)S(1)} %broadcast_multiply_fusion.1), kind=kOutput, calls=%fused_computation.30 | convolution fusion | flops 4535894016 | bytes 13579776 | tf_op jit(solution)/shard_map/nd,nf->df/dot_general | solution.py:200
  405.8 5.6 reshape.786
  411.4 6.1 copy.112
  417.4 11.3 %convert_reduce_fusion.1 = (f32[12,64]{1,0:T(8,128)S(1)}, bf16[3,12,64,320]{3,2,1,0:T(8,128)(2,1)}) fusion(bf16[3,320,12,64]{1,3,2,0:T(8,128)(2,1)S(1)} %copy.112, f32[3,12,320,320]{2,3,1,0:T(8,128)} %get-tuple-element.129, f32[3,12,320]{2,1,0:T(8,128)S(1)} %log_add_fusion, pred[3,320,320]{1,2,0:T(8,128)(4,1)S(1)} %broadcast_compare_fusion), kind=kOutput, calls=%fused_computation.37 | convolution fusion | flops 488815872 | bytes 18051072 | tf_op jit(solution)/shard_map/shqk,sqhd->skhd/dot_general | solution.py:241
  428.8 12.8 %multiply_reduce_fusion = (f32[3,12,320]{2,1,0:T(8,128)S(1)}, f32[3,12,320,320]{2,3,1,0:T(8,128)}) fusion(f32[3,12,320,320]{2,3,1,0:T(8,128)} %get-tuple-element.129, f32[3,12,320]{2,1,0:T(8,128)S(1)} %log_add_fusion, pred[3,320,320]{1,2,0:T(8,128)(4,1)S(1)} %broadcast_compare_fusion, bf16[3,320,12,64]{1,3,2,0:T(8,128)(2,1)S(1)} %copy.112, ...), kind=kOutput, calls=%fused_computation.1 | convolution fusion | flops 490279680 | bytes 32839680 | tf_op jit(solution)/shard_map/sqhd,skhd->shqk/dot_general | solution.py:222
  441.6 12.9 %multiply_convert_fusion = bf16[3,12,320,320]{2,3,1,0:T(8,128)(2,1)S(1)} fusion(f32[3,12,320,320]{2,3,1,0:T(8,128)} %get-tuple-element.135, f32[3,12,320,320]{2,3,1,0:T(8,128)} %get-tuple-element.129, f32[3,12,320]{2,1,0:T(8,128)S(1)} %get-tuple-element.134, f32[3,12,320]{2,1,0:T(8,128)S(1)} %log_add_fusion, pred[3,320,320]{1,2,0:T(8,128)(4,1)S(1)} %broadcast_compare_fusion), kind=kLoop, calls=%fused_computation | loop fusion | flops 22118400 | bytes 37263360 | tf_op jit(solution)/shard_map/convert_element_type | solution.py:226
  463.7 5.4 convert_element_type.701
  472.1 5.4 convert_element_type.697
  491.8 6.3 multiply_reduce_fusion.2
  498.1 5.7 convolution_convert_fusion
  521.4 8.9 %multiply_convert_fusion.5 = bf16[960,768]{1,0:T(8,128)(2,1)S(1)} fusion(f32[960,768]{1,0:T(8,128)S(1)} %copy-done.8, bf16[960,3072]{1,0:T(8,128)(2,1)} %get-tuple-element.35, bf16[3072,384]{1,0:T(8,128)(2,1)} %bitcast.572, bf16[3072,384]{1,0:T(8,128)(2,1)} %bitcast.104, f32[768]{0:T(1024)S(1)} %copy-done.99, f32[960]{0:T(1024)S(1)} %copy-done.89), kind=kOutput, calls=%fused_computation.60 | convolution fusion | flops 4542234624 | bytes 15047424 | tf_op jit(solution)/shard_map/dot_general | solution.py:188
  563.1 7.9 %collective-permute-done.62 = bf16[3,80,768]{2,1,0:T(8,128)(2,1)S(1)} collective-permute-done((bf16[3,80,768]{2,1,0:T(8,128)(2,1)S(1)}, bf16[3,80,768]{2,1,0:T(8,128)(2,1)S(1)}, u32[]{:S(2)}, u32[]{:S(2)}) %collective-permute-start.62) | collective-permute-done | bytes 368672 | tf_op jit(solution)/shard_map/ppermute | solution.py:31
  573.4 5.5 collective-permute-done.55
  616.0 5.6 collective-permute-done.70
  625.2 14.7 %collective-permute-done.71 = bf16[4,24,1152]{2,1,0:T(8,128)(2,1)S(1)} collective-permute-done((bf16[4,24,1152]{2,1,0:T(8,128)(2,1)S(1)}, bf16[4,24,1152]{2,1,0:T(8,128)(2,1)S(1)}, u32[]{:S(2)}, u32[]{:S(2)}) %collective-permute-start.71) | collective-permute-done | bytes 221216 | tf_op jit(solution)/shard_map/ppermute | solution.py:31
  658.2 9.0 %collective-permute-done.94 = bf16[4,2,24,1536]{3,2,0,1:T(8,128)(2,1)S(1)} collective-permute-done((bf16[4,2,24,1536]{3,2,0,1:T(8,128)(2,1)S(1)}, bf16[4,2,24,1536]{3,2,0,1:T(8,128)(2,1)S(1)}, u32[]{:S(2)}, u32[]{:S(2)}) %collective-permute-start.94) | collective-permute-done | bytes 589856 | tf_op jit(solution)/shard_map/ppermute | solution.py:31
  (731 shorter events, 395.1 us)
Async XLA Ops:
  2.3 41.5 %collective-permute-start.12 = (bf16[24,1152]{1,0:T(8,128)(2,1)}, bf16[24,1152]{1,0:T(8,128)(2,1)}, u32[]{:S(2)}, u32[]{:S(2)}) collective-permute-start(bf16[24,1152]{1,0:T(8,128)(2,1)} %slice.179), channel_id=1, source_target_pairs={{0,2},{1,3},{2,0},{3,1},{4,6},{5,7},{6,4},{7,5},{8,10},{9,11},{10,... | collective-permute-start | bytes 165896 | tf_op jit(solution)/shard_map/ppermute | solution.py:31
  5.3 40.9 %collective-permute-start.13 = (bf16[24,1152]{1,0:T(8,128)(2,1)}, bf16[24,1152]{1,0:T(8,128)(2,1)}, u32[]{:S(2)}, u32[]{:S(2)}) collective-permute-start(bf16[24,1152]{1,0:T(8,128)(2,1)} %slice.179), channel_id=1, source_target_pairs={{0,4},{1,5},{2,6},{3,7},{4,0},{5,1},{6,2},{7,3},{8,12},{9,13},{10,... | collective-permute-start | bytes 165896 | tf_op jit(solution)/shard_map/ppermute | solution.py:31
  24.9 22.6 %collective-permute-start.14 = (bf16[24,1152]{1,0:T(8,128)(2,1)}, bf16[24,1152]{1,0:T(8,128)(2,1)S(1)}, u32[]{:S(2)}, u32[]{:S(2)}) collective-permute-start(bf16[24,1152]{1,0:T(8,128)(2,1)} %slice.179), channel_id=1, source_target_pairs={{0,6},{1,7},{2,4},{3,5},{4,2},{5,3},{6,0},{7,1},{8,14},{9,15},{10,... | collective-permute-start | bytes 165896 | tf_op jit(solution)/shard_map/ppermute | solution.py:31
  75.6 77.7 %collective-permute-start.3 = (bf16[3,80,768]{2,1,0:T(8,128)(2,1)S(1)}, bf16[3,80,768]{2,1,0:T(8,128)(2,1)S(1)}, u32[]{:S(2)}, u32[]{:S(2)}) collective-permute-start(bf16[3,80,768]{2,1,0:T(8,128)(2,1)S(1)} %copy-done.81), channel_id=1, source_target_pairs={{0,8},{1,9},{2,10},{3,11},{4,12},{5,13},{6,14},{7,15},{8,0},{9,1},... | collective-permute-start | bytes 1105928 | tf_op jit(solution)/shard_map/ppermute | solution.py:31
  75.7 77.6 %collective-permute-start.4 = (bf16[3,80,768]{2,1,0:T(8,128)(2,1)S(1)}, bf16[3,80,768]{2,1,0:T(8,128)(2,1)S(1)}, u32[]{:S(2)}, u32[]{:S(2)}) collective-permute-start(bf16[3,80,768]{2,1,0:T(8,128)(2,1)S(1)} %copy-done.79), channel_id=1, source_target_pairs={{0,16},{1,17},{2,18},{3,19},{4,20},{5,21},{6,22},{7,23},{8,24},{9,... | collective-permute-start | bytes 1105928 | tf_op jit(solution)/shard_map/ppermute | solution.py:31
  77.5 76.5 %collective-permute-start.5 = (bf16[3,80,768]{2,1,0:T(8,128)(2,1)S(1)}, bf16[3,80,768]{2,1,0:T(8,128)(2,1)S(1)}, u32[]{:S(2)}, u32[]{:S(2)}) collective-permute-start(bf16[3,80,768]{2,1,0:T(8,128)(2,1)S(1)} %copy-done.77), channel_id=1, source_target_pairs={{0,24},{1,25},{2,26},{3,27},{4,28},{5,29},{6,30},{7,31},{8,16},{9,... | collective-permute-start | bytes 1105928 | tf_op jit(solution)/shard_map/ppermute | solution.py:31
  77.9 77.0 %collective-permute-start.57 = (bf16[3,80,768]{2,1,0:T(8,128)(2,1)S(1)}, bf16[3,80,768]{2,1,0:T(8,128)(2,1)S(1)}, u32[]{:S(2)}, u32[]{:S(2)}) collective-permute-start(bf16[3,80,768]{2,1,0:T(8,128)(2,1)S(1)} %copy-done.82), channel_id=1, source_target_pairs={{0,8},{1,9},{2,10},{3,11},{4,12},{5,13},{6,14},{7,15},{8,0},{9,1},... | collective-permute-start | bytes 1105928 | tf_op jit(solution)/shard_map/ppermute | solution.py:31
  153.9 18.4 %collective-permute-start.23 = (bf16[2,4,2,24,384]{4,3,2,1,0:T(8,128)(2,1)}, bf16[2,4,2,24,384]{4,3,2,1,0:T(8,128)(2,1)}, u32[]{:S(2)}, u32[]{:S(2)}) collective-permute-start(bf16[2,4,2,24,384]{4,3,2,1,0:T(8,128)(2,1)} %bitcast_dynamic-update-slice_fusion.43), channel_id=1, source_target_pairs={{0,8},{1,9},{2,10},{3,11},{4,12},{5,13},{6,14},{7,15},{8,0},{9,1},... | collective-permute-start | bytes 884744 | tf_op jit(solution)/shard_map/ppermute | solution.py:31
  155.0 21.1 %collective-permute-start.16 = (bf16[2,4,24,1152]{3,2,1,0:T(8,128)(2,1)}, bf16[2,4,24,1152]{3,2,1,0:T(8,128)(2,1)}, u32[]{:S(2)}, u32[]{:S(2)}) collective-permute-start(bf16[2,4,24,1152]{3,2,1,0:T(8,128)(2,1)} %bitcast_dynamic-update-slice_fusion.38), channel_id=1, source_target_pairs={{0,1},{1,0},{2,3},{3,2},{4,5},{5,4},{6,7},{7,6},{8,9},{9,8},{10,11... | collective-permute-start | bytes 1327112 | tf_op jit(solution)/shard_map/ppermute | solution.py:31
  157.9 22.0 %collective-permute-start.10 = (bf16[4,2,24,1280]{3,2,1,0:T(8,128)(2,1)}, bf16[4,2,24,1280]{3,2,1,0:T(8,128)(2,1)}, u32[]{:S(2)}, u32[]{:S(2)}) collective-permute-start(bf16[4,2,24,1280]{3,2,1,0:T(8,128)(2,1)} %bitcast_dynamic-update-slice_fusion.37), channel_id=1, source_target_pairs={{0,16},{1,17},{2,18},{3,19},{4,20},{5,21},{6,22},{7,23},{8,24},{9,... | collective-permute-start | bytes 1474568 | tf_op jit(solution)/shard_map/ppermute | solution.py:31
  165.8 23.3 %collective-permute-start.40 = (bf16[4,2,24,1536]{3,2,1,0:T(8,128)(2,1)}, bf16[4,2,24,1536]{3,2,1,0:T(8,128)(2,1)}, u32[]{:S(2)}, u32[]{:S(2)}) collective-permute-start(bf16[4,2,24,1536]{3,2,1,0:T(8,128)(2,1)} %bitcast_dynamic-update-slice_fusion.26), channel_id=1, source_target_pairs={{0,16},{1,17},{2,18},{3,19},{4,20},{5,21},{6,22},{7,23},{8,24},{9,... | collective-permute-start | bytes 1769480 | tf_op jit(solution)/shard_map/ppermute | solution.py:31
  169.1 32.6 %collective-permute-start.34 = (bf16[2,4,24,1536]{3,2,1,0:T(8,128)(2,1)}, bf16[2,4,24,1536]{3,2,1,0:T(8,128)(2,1)S(1)}, u32[]{:S(2)}, u32[]{:S(2)}) collective-permute-start(bf16[2,4,24,1536]{3,2,1,0:T(8,128)(2,1)} %copy-done.50), channel_id=1, source_target_pairs={{0,1},{1,0},{2,3},{3,2},{4,5},{5,4},{6,7},{7,6},{8,9},{9,8},{10,11... | collective-permute-start | bytes 1769480 | tf_op jit(solution)/shard_map/ppermute | solution.py:31
  172.3 28.5 %collective-permute-start.52 = (bf16[4,2,96,384]{3,2,1,0:T(8,128)(2,1)}, bf16[4,2,96,384]{3,2,1,0:T(8,128)(2,1)S(1)}, u32[]{:S(2)}, u32[]{:S(2)}) collective-permute-start(bf16[4,2,96,384]{3,2,1,0:T(8,128)(2,1)} %copy-done.51), channel_id=1, source_target_pairs={{0,16},{1,17},{2,18},{3,19},{4,20},{5,21},{6,22},{7,23},{8,24},{9,... | collective-permute-start | bytes 1769480 | tf_op jit(solution)/shard_map/ppermute | solution.py:31
  176.1 31.3 %collective-permute-start.46 = (bf16[2,4,96,384]{3,2,1,0:T(8,128)(2,1)}, bf16[2,4,96,384]{3,2,1,0:T(8,128)(2,1)S(1)}, u32[]{:S(2)}, u32[]{:S(2)}) collective-permute-start(bf16[2,4,96,384]{3,2,1,0:T(8,128)(2,1)} %copy-done.52), channel_id=1, source_target_pairs={{0,1},{1,0},{2,3},{3,2},{4,5},{5,4},{6,7},{7,6},{8,9},{9,8},{10,11... | collective-permute-start | bytes 1769480 | tf_op jit(solution)/shard_map/ppermute | solution.py:31
  179.9 34.5 %collective-permute-start.17 = (bf16[2,4,2,24,1152]{4,3,2,1,0:T(8,128)(2,1)S(1)}, bf16[2,4,2,24,1152]{4,3,2,1,0:T(8,128)(2,1)S(1)}, u32[]{:S(2)}, u32[]{:S(2)}) collective-permute-start(bf16[2,4,2,24,1152]{4,3,2,1,0:T(8,128)(2,1)S(1)} %copy-done.38), channel_id=1, source_target_pairs={{0,8},{1,9},{2,10},{3,11},{4,12},{5,13},{6,14},{7,15},{8,0},{9,1},... | collective-permute-start | bytes 2654216 | tf_op jit(solution)/shard_map/ppermute | solution.py:31
  189.1 26.1 %collective-permute-start.11 = (bf16[2,4,2,24,1280]{4,3,2,1,0:T(8,128)(2,1)S(1)}, bf16[2,4,2,24,1280]{4,3,2,1,0:T(8,128)(2,1)S(1)}, u32[]{:S(2)}, u32[]{:S(2)}) collective-permute-start(bf16[2,4,2,24,1280]{4,3,2,1,0:T(8,128)(2,1)S(1)} %bitcast_dynamic-update-slice_fusion.20), channel_id=1, source_target_pairs={{0,8},{1,9},{2,10},{3,11},{4,12},{5,13},{6,14},{7,15},{8,0},{9,1},... | collective-permute-start | bytes 2949128 | tf_op jit(solution)/shard_map/ppermute | solution.py:31
  200.8 119.1 %collective-permute-start.41 = (bf16[2,4,2,24,1536]{4,3,2,1,0:T(8,128)(2,1)}, bf16[2,4,2,24,1536]{4,3,2,1,0:T(8,128)(2,1)}, u32[]{:S(2)}, u32[]{:S(2)}) collective-permute-start(bf16[2,4,2,24,1536]{4,3,2,1,0:T(8,128)(2,1)} %bitcast_dynamic-update-slice_fusion.17), channel_id=1, source_target_pairs={{0,8},{1,9},{2,10},{3,11},{4,12},{5,13},{6,14},{7,15},{8,0},{9,1},... | collective-permute-start | bytes 3538952 | tf_op jit(solution)/shard_map/ppermute | solution.py:31
  201.7 159.9 %collective-permute-start.53 = (bf16[2,4,2,96,384]{4,3,2,1,0:T(8,128)(2,1)}, bf16[2,4,2,96,384]{4,3,2,1,0:T(8,128)(2,1)}, u32[]{:S(2)}, u32[]{:S(2)}) collective-permute-start(bf16[2,4,2,96,384]{4,3,2,1,0:T(8,128)(2,1)} %bitcast_dynamic-update-slice_fusion.14), channel_id=1, source_target_pairs={{0,8},{1,9},{2,10},{3,11},{4,12},{5,13},{6,14},{7,15},{8,0},{9,1},... | collective-permute-start | bytes 3538952 | tf_op jit(solution)/shard_map/ppermute | solution.py:31
  207.4 116.0 %collective-permute-start.35 = (bf16[2,4,2,24,1536]{4,3,2,1,0:T(8,128)(2,1)}, bf16[2,4,2,24,1536]{4,3,2,1,0:T(8,128)(2,1)}, u32[]{:S(2)}, u32[]{:S(2)}) collective-permute-start(bf16[2,4,2,24,1536]{4,3,2,1,0:T(8,128)(2,1)} %bitcast_dynamic-update-slice_fusion.19), channel_id=1, source_target_pairs={{0,8},{1,9},{2,10},{3,11},{4,12},{5,13},{6,14},{7,15},{8,0},{9,1},... | collective-permute-start | bytes 3538952 | tf_op jit(solution)/shard_map/ppermute | solution.py:31
  214.4 148.8 %collective-permute-start.47 = (bf16[2,4,2,96,384]{4,3,2,1,0:T(8,128)(2,1)}, bf16[2,4,2,96,384]{4,3,2,1,0:T(8,128)(2,1)}, u32[]{:S(2)}, u32[]{:S(2)}) collective-permute-start(bf16[2,4,2,96,384]{4,3,2,1,0:T(8,128)(2,1)} %bitcast_dynamic-update-slice_fusion.16), channel_id=1, source_target_pairs={{0,8},{1,9},{2,10},{3,11},{4,12},{5,13},{6,14},{7,15},{8,0},{9,1},... | collective-permute-start | bytes 3538952 | tf_op jit(solution)/shard_map/ppermute | solution.py:31
  507.5 103.0 %collective-permute-start.105 = (bf16[2,4,2,96,384]{4,3,1,2,0:T(8,128)(2,1)}, bf16[2,4,2,96,384]{4,3,1,2,0:T(8,128)(2,1)}, u32[]{:S(2)}, u32[]{:S(2)}) collective-permute-start(bf16[2,4,2,96,384]{4,3,1,2,0:T(8,128)(2,1)} %bitcast.548), channel_id=1, source_target_pairs={{0,8},{1,9},{2,10},{3,11},{4,12},{5,13},{6,14},{7,15},{8,0},{9,1},... | collective-permute-start | bytes 3538952 | tf_op jit(solution)/shard_map/ppermute | solution.py:31
  514.2 22.5 %collective-permute-start.63 = (f32[2,4,2,1,288]{4,3,2,1,0:T(1,128)S(1)}, f32[2,4,2,1,288]{4,3,2,1,0:T(1,128)S(1)}, u32[]{:S(2)}, u32[]{:S(2)}) collective-permute-start(f32[2,4,2,1,288]{4,3,2,1,0:T(1,128)S(1)} %fusion.70), channel_id=1, source_target_pairs={{0,8},{1,9},{2,10},{3,11},{4,12},{5,13},{6,14},{7,15},{8,0},{9,1},... | collective-permute-start | bytes 55304 | tf_op jit(solution)/shard_map/ppermute | solution.py:31
  556.3 22.6 %collective-permute-start.55 = (bf16[3,80,768]{2,1,0:T(8,128)(2,1)S(1)}, bf16[3,80,768]{2,1,0:T(8,128)(2,1)S(1)}, u32[]{:S(2)}, u32[]{:S(2)}) collective-permute-start(bf16[3,80,768]{2,1,0:T(8,128)(2,1)S(1)} %get-tuple-element.70), channel_id=1, source_target_pairs={{0,16},{1,17},{2,18},{3,19},{4,20},{5,21},{6,22},{7,23},{8,24},{9,... | collective-permute-start | bytes 1105928 | tf_op jit(solution)/shard_map/ppermute | solution.py:31
  563.1 21.9 %collective-permute-start.56 = (bf16[3,80,768]{2,1,0:T(8,128)(2,1)S(1)}, bf16[3,80,768]{2,1,0:T(8,128)(2,1)S(1)}, u32[]{:S(2)}, u32[]{:S(2)}) collective-permute-start(bf16[3,80,768]{2,1,0:T(8,128)(2,1)S(1)} %get-tuple-element.69), channel_id=1, source_target_pairs={{0,24},{1,25},{2,26},{3,27},{4,28},{5,29},{6,30},{7,31},{8,16},{9,... | collective-permute-start | bytes 1105928 | tf_op jit(solution)/shard_map/ppermute | solution.py:31
  571.0 35.9 %collective-permute-start.69 = (bf16[2,4,2,24,1152]{4,3,1,2,0:T(8,128)(2,1)S(1)}, bf16[2,4,2,24,1152]{4,3,1,2,0:T(8,128)(2,1)S(1)}, u32[]{:S(2)}, u32[]{:S(2)}) collective-permute-start(bf16[2,4,2,24,1152]{4,3,1,2,0:T(8,128)(2,1)S(1)} %bitcast.587), channel_id=1, source_target_pairs={{0,8},{1,9},{2,10},{3,11},{4,12},{5,13},{6,14},{7,15},{8,0},{9,1},... | collective-permute-start | bytes 2654216 | tf_op jit(solution)/shard_map/ppermute | solution.py:31
  613.8 41.7 %collective-permute-start.106 = (bf16[4,2,96,384]{3,2,0,1:T(8,128)(2,1)S(1)}, bf16[4,2,96,384]{3,2,0,1:T(8,128)(2,1)S(1)}, u32[]{:S(2)}, u32[]{:S(2)}) collective-permute-start(bf16[4,2,96,384]{3,2,0,1:T(8,128)(2,1)S(1)} %dynamic-slice_bitcast_fusion.1), channel_id=1, source_target_pairs={{0,16},{1,17},{2,18},{3,19},{4,20},{5,21},{6,22},{7,23},{8,24},{9,... | collective-permute-start | bytes 1769480 | tf_op jit(solution)/shard_map/ppermute | solution.py:31
  614.8 42.6 %collective-permute-start.112 = (bf16[2,4,96,384]{3,2,1,0:T(8,128)(2,1)S(1)}, bf16[2,4,96,384]{3,2,1,0:T(8,128)(2,1)S(1)}, u32[]{:S(2)}, u32[]{:S(2)}) collective-permute-start(bf16[2,4,96,384]{3,2,1,0:T(8,128)(2,1)S(1)} %dynamic-slice_bitcast_fusion), channel_id=1, source_target_pairs={{0,1},{1,0},{2,3},{3,2},{4,5},{5,4},{6,7},{7,6},{8,9},{9,8},{10,11... | collective-permute-start | bytes 1769480 | tf_op jit(solution)/shard_map/ppermute | solution.py:31
  621.8 18.0 %collective-permute-start.71 = (bf16[4,24,1152]{2,1,0:T(8,128)(2,1)S(1)}, bf16[4,24,1152]{2,1,0:T(8,128)(2,1)S(1)}, u32[]{:S(2)}, u32[]{:S(2)}) collective-permute-start(bf16[4,24,1152]{2,1,0:T(8,128)(2,1)S(1)} %dynamic-slice_bitcast_fusion.11), channel_id=1, source_target_pairs={{0,1},{1,0},{2,3},{3,2},{4,5},{5,4},{6,7},{7,6},{8,9},{9,8},{10,11... | collective-permute-start | bytes 663560 | tf_op jit(solution)/shard_map/ppermute | solution.py:31
  623.7 18.6 %collective-permute-start.77 = (bf16[4,24,1152]{2,1,0:T(8,128)(2,1)S(1)}, bf16[4,24,1152]{2,1,0:T(8,128)(2,1)S(1)}, u32[]{:S(2)}, u32[]{:S(2)}) collective-permute-start(bf16[4,24,1152]{2,1,0:T(8,128)(2,1)S(1)} %dynamic-slice_bitcast_fusion.10), channel_id=1, source_target_pairs={{0,16},{1,17},{2,18},{3,19},{4,20},{5,21},{6,22},{7,23},{8,24},{9,... | collective-permute-start | bytes 663560 | tf_op jit(solution)/shard_map/ppermute | solution.py:31
  651.4 17.6 %collective-permute-start.100 = (bf16[2,4,24,1536]{3,2,1,0:T(8,128)(2,1)S(1)}, bf16[2,4,24,1536]{3,2,1,0:T(8,128)(2,1)S(1)}, u32[]{:S(2)}, u32[]{:S(2)}) collective-permute-start(bf16[2,4,24,1536]{3,2,1,0:T(8,128)(2,1)S(1)} %dynamic-slice_bitcast_fusion.2), channel_id=1, source_target_pairs={{0,1},{1,0},{2,3},{3,2},{4,5},{5,4},{6,7},{7,6},{8,9},{9,8},{10,11... | collective-permute-start | bytes 1769480 | tf_op jit(solution)/shard_map/ppermute | solution.py:31
  655.7 17.0 %collective-permute-start.107 = (bf16[4,96,384]{2,1,0:T(8,128)(2,1)S(1)}, bf16[4,96,384]{2,1,0:T(8,128)(2,1)S(1)}, u32[]{:S(2)}, u32[]{:S(2)}) collective-permute-start(bf16[4,96,384]{2,1,0:T(8,128)(2,1)S(1)} %dynamic-slice_bitcast_fusion.7), channel_id=1, source_target_pairs={{0,1},{1,0},{2,3},{3,2},{4,5},{5,4},{6,7},{7,6},{8,9},{9,8},{10,11... | collective-permute-start | bytes 884744 | tf_op jit(solution)/shard_map/ppermute | solution.py:31
  657.6 17.5 %collective-permute-start.113 = (bf16[4,96,384]{2,1,0:T(8,128)(2,1)S(1)}, bf16[4,96,384]{2,1,0:T(8,128)(2,1)S(1)}, u32[]{:S(2)}, u32[]{:S(2)}) collective-permute-start(bf16[4,96,384]{2,1,0:T(8,128)(2,1)S(1)} %dynamic-slice_bitcast_fusion.6), channel_id=1, source_target_pairs={{0,16},{1,17},{2,18},{3,19},{4,20},{5,21},{6,22},{7,23},{8,24},{9,... | collective-permute-start | bytes 884744 | tf_op jit(solution)/shard_map/ppermute | solution.py:31
  (191 other events, 2453.7 us)

commit v2 on v1

--- a/solution.py
+++ b/solution.py
@@ -39,40 +39,70 @@
     return lax.dynamic_index_in_dim(value, index, axis, keepdims=False)
 
 
-def gather_axis(grid, here, value, name, axis):
-    count = grid.sizes[name]
-    parts = [value] + [grid.swap(value, **{name: bits}) for bits in range(1, count)]
-    shape = value.shape[:axis] + (count,) + value.shape[axis:]
-    buffer = jnp.zeros(shape, value.dtype)
-    for bits, part in enumerate(parts):
-        buffer = put(buffer, part, axis, here[name] ^ bits)
-    return buffer
-
-
-def gather_weight(grid, here, shard, order):
-    have = []
-    value = shard
-    for name in order:
-        axis = sum(1 for done in have if "x core z y".split().index(done) < "x core z y".split().index(name))
-        value = gather_axis(grid, here, value, name, axis)
-        have.append(name)
-    return value.reshape((-1,) + shard.shape[1:])
-
-
-def scatter_weight(grid, here, grad, order, keep=jnp.bfloat16):
+def mixed_swap(grid, value, first):
+    pairs = []
+    for index in range(grid.frames * grid.clips):
+        frame, clip = divmod(index, grid.clips)
+        if frame % 2 == first:
+            frame ^= 2
+        else:
+            clip ^= 1
+        pairs.append((index, frame * grid.clips + clip))
+    return lax.ppermute(value, AXES, pairs)
+
+
+def cell(here, core, near, far):
+    x = jnp.where(core == 0, here["x"] ^ near, here["x"] ^ far)
+    y = jnp.where(core == 0, here["y"] ^ far, here["y"] ^ near)
+    return x, y
+
+
+def gather_group(grid, here, shard):
+    count = grid.sizes["z"]
+    rows, width = shard.shape
+    column = jnp.zeros((count, rows, width), shard.dtype)
+    for bits in range(count):
+        part = grid.swap(shard, z=bits) if bits else shard
+        column = put(column, part, 0, here["z"] ^ bits)
+    pair = jnp.stack([column, mixed_swap(grid, column, 0)])
+    other = mixed_swap(grid, pair, 1)
+    halves = ((pair, other), (grid.swap(pair, core=1), grid.swap(other, core=1)))
+    full = jnp.zeros((grid.sizes["x"], 2, count, 2, rows, width), shard.dtype)
+    for side in range(2):
+        core = here["core"] ^ side
+        for far in range(2):
+            for near in range(2):
+                x, y = cell(here, core, near, far)
+                piece = halves[side][far][near][None, None, :, None]
+                full = lax.dynamic_update_slice(full, piece, (x, core, 0, y, 0, 0))
+    return full.reshape(-1, width)
+
+
+def scatter_group(grid, here, grad):
     sizes = grid.sizes
+    count = sizes["z"]
+    width = grad.shape[1]
     rows = grad.shape[0] // (grid.frames * grid.clips)
-    value = grad.reshape((sizes["x"], sizes["core"], sizes["z"], sizes["y"], rows) + grad.shape[1:])
-    left = ["x", "core", "z", "y"]
-    for step, name in enumerate(order):
-        axis = left.index(name)
-        total = pick(value, axis, here[name]).astype(jnp.float32)
-        for bits in range(1, sizes[name]):
-            sent = pick(value, axis, here[name] ^ bits)
-            total = total + grid.swap(sent, **{name: bits}).astype(jnp.float32)
-        left.remove(name)
-        value = total if step == len(order) - 1 else total.astype(keep)
-    return value
+    core = here["core"]
+    value = grad.reshape((sizes["x"], 2, count, 2, rows, width))
+    value = pick(value, 1, core).astype(jnp.float32) + grid.swap(pick(value, 1, 1 - core), core=1).astype(jnp.float32)
+    value = value.astype(jnp.bfloat16)
+
+    def piece(near, far):
+        x = jnp.where(core == 0, here["x"] ^ near, far)
+        y = jnp.where(core == 0, far, here["y"] ^ near)
+        return lax.dynamic_slice(value, (x, 0, y, 0, 0), (1, count, 1, rows, width))[0, :, 0]
+
+    sent = jnp.stack([piece(1, 0), piece(1, 1)])
+    kept = jnp.stack([piece(0, 0), piece(0, 1)])
+    value = (kept.astype(jnp.float32) + mixed_swap(grid, sent, 0).astype(jnp.float32)).astype(jnp.bfloat16)
+    own = jnp.where(core == 0, here["y"], here["x"])
+    value = pick(value, 0, own).astype(jnp.float32) + mixed_swap(grid, pick(value, 0, 1 - own), 1).astype(jnp.float32)
+    value = value.astype(jnp.bfloat16)
+    total = pick(value, 0, here["z"]).astype(jnp.float32)
+    for bits in range(1, count):
+        total = total + grid.swap(pick(value, 0, here["z"] ^ bits), z=bits).astype(jnp.float32)
+    return total
 
 
 def to_slots(grid, here, value):
@@ -316,22 +346,23 @@
     small = jnp.pad(small, ((0, 0), (0, 128 - small.shape[1])))
     token_rows = to_slots(grid, here, tokens)
 
-    def gathered(shard):
-        width = shard.shape[1]
-        half = (width // 256) * 128
-        left = gather_weight(grid, here, shard[:, :half], ("z", "x", "y", "core"))
-        right = gather_weight(grid, here, shard[:, half:], ("z", "y", "x", "core"))
-        return jnp.concatenate([left, right], axis=1)
-
-    mixed = gathered(jnp.concatenate([w_qkv, small], axis=1))
+    mixed = gather_group(grid, here, jnp.concatenate([w_qkv, small], axis=1))
+    down_rows = w_down.reshape(ratio, rows, w_down.shape[1])
+    rest = gather_group(
+        grid, here, jnp.concatenate([w_out, w_up] + [down_rows[i] for i in range(ratio)], axis=1)
+    )
     qkv_full = mixed[:, : w_qkv.shape[1]]
     small_full = mixed[:, w_qkv.shape[1] :]
     vectors = [small_full[:, i] for i in range(8)]
     up_bias_full = small_full[:, 8 : 8 + ratio].reshape(-1)
-    out_full = gathered(w_out)
-    up_full = gathered(w_up)
+    model, hidden = w_out.shape[1], w_up.shape[1]
+    devices = grid.frames * grid.clips
+    out_full = rest[:, :model]
+    up_full = rest[:, model : model + hidden]
+    down_full = (
+        rest[:, model + hidden :].reshape(devices, rows, ratio, model).transpose(0, 2, 1, 3).reshape(-1, model)
+    )
     cotangent_rows = to_slots(grid, here, cotangent)
-    down_full = gathered(w_down)
     full = (
         vectors[0], vectors[1], qkv_full, vectors[2], vectors[3], out_full, vectors[4],
         vectors[5], vectors[6], up_full, up_bias_full, down_full, vectors[7],
@@ -342,27 +373,27 @@
     output = from_slots(grid, here, output_rows)
     input_grad = from_slots(grid, here, input_rows.astype(jnp.bfloat16)).astype(jnp.float32)
 
-    def scattered(grad):
-        low = grad.astype(jnp.bfloat16)
-        half = (grad.shape[1] // 256) * 128
-        left = scatter_weight(grid, here, low[:, :half], ("core", "x", "y", "z"))
-        right = scatter_weight(grid, here, low[:, half:], ("core", "y", "x", "z"))
-        return jnp.concatenate([left, right], axis=1)
-
-    g_down = scattered(grads[11])
-    g_up = scattered(grads[9])
-    g_out = scattered(grads[5])
-    g_qkv = scattered(grads[2])
-    devices = grid.frames * grid.clips
+    def low(grad):
+        return grad.astype(jnp.bfloat16)
+
+    g_down = scatter_group(
+        grid,
+        here,
+        low(grads[11]).reshape(devices, ratio, rows, model).transpose(0, 2, 1, 3).reshape(devices * rows, ratio * model),
+    )
+    g_down = g_down.reshape(rows, ratio, model).transpose(1, 0, 2).reshape(ratio * rows, model)
+    g_up = scatter_group(grid, here, low(grads[9]))
+    g_qkv = scatter_group(grid, here, low(grads[2]))
     order = (0, 1, 3, 4, 6, 7, 8, 12)
-    pack = jnp.concatenate(
-        [grads[i].reshape(devices, rows) for i in order] + [grads[10].reshape(devices, rows * ratio)], axis=1
-    )
-    pack = scatter_weight(grid, here, pack, ("core", "x", "y", "z"), jnp.float32)[0]
-    v = {g: pack[i * rows : (i + 1) * rows] for i, g in enumerate(order)}
+    pack = jnp.concatenate([jnp.stack([grads[i] for i in order], axis=1), grads[10].reshape(-1, ratio)], axis=1)
+    pack = jnp.pad(low(pack), ((0, 0), (0, 128 - pack.shape[1])))
+    last = scatter_group(grid, here, jnp.concatenate([low(grads[5]), pack], axis=1))
+    g_out = last[:, :model]
+    v = {g: last[:, model + i] for i, g in enumerate(order)}
+    g_up_bias = last[:, model + 8 : model + 8 + ratio].reshape(-1)
     return (
         output, input_grad, v[0], v[1], g_qkv, v[3], v[4], g_out, v[6], v[7], v[8],
-        g_up, pack[8 * rows :], g_down, v[12],
+        g_up, g_up_bias, g_down, v[12],
     )
 
 

time: 712 us -> 633 us (0.89)
  starting transfers between devices: 141 us -> 61.2 us
  waiting for transfers between devices: 146 us -> 102 us
  other arithmetic: 53.7 us -> 72.8 us
  matrix products: 158 us -> 175 us
  local copies, waits for them, and re-layouts: 199 us -> 209 us
    ppermute x117 -> x41, waiting for transfers between devices: 146 us -> 44.2 us  [swap(): return lax.ppermute(value, AXES, pairs)]
    ppermute x117 -> x41, starting transfers between devices: 141 us -> 46.6 us  [swap(): return lax.ppermute(value, AXES, pairs)]
    ppermute x0 -> x12, waiting for transfers between devices: none -> 57.7 us  [mixed_swap(): return lax.ppermute(value, AXES, pairs)]
    dynamic_update_slice x79 -> x7, local copies, waits for them, and re-layouts: 53.3 us -> 5.96 us  [put(): return lax.dynamic_update_index_in_dim(buffer, piece, index, axis)]
    dot_general x1, matrix products: 35.8 us -> 8.68 us  [layer_step(): jnp.dot(second_low, w_up, preferred_element_type=jnp.float32)]
    dynamic_update_slice x0 -> x16, local copies, waits for them, and re-layouts: none -> 26.1 us  [gather_group(): full = lax.dynamic_update_slice(full, piece, (x, core, 0, y, 0, 0))]
    reshape x0 -> x7, local copies, waits for them, and re-layouts: none -> 18.9 us  [the longest x2 13.2 us: body(): rest[:, model + hidden:].reshape(devices, rows, ratio, model)]
    dot_general x1, matrix products: 15.3 us -> 32.9 us  [layer_step(): jnp.einsum('nd,fd->nf', grad_low, w_down, preferred_element_type=jnp.floa...]
  transfers between devices with their start and end apart: 117 -> 53, of which waited for: 44 -> 17; matrix products, arithmetic and copies ran while one was open for 37% -> 35% of each run, Pallas kernels for 0% -> 0%
where the time goes in v2:
time: 633 us; the launch traced here: 621 us
  local copies, waits for them, and re-layouts  209 us (33%)
  matrix products  175 us (28%)
  waiting for transfers between devices  102 us (16%)
  other arithmetic  72.8 us (12%)
  starting transfers between devices  61.2 us (10%)
    ppermute x12, waiting for transfers between devices, mixed_swap(): return lax.ppermute(value, AXES, pairs)  57.7 us
    ppermute x41, starting transfers between devices, swap(): return lax.ppermute(value, AXES, pairs)  46.6 us
    ppermute x41, waiting for transfers between devices, swap(): return lax.ppermute(value, AXES, pairs)  44.2 us
    dot_general x1, matrix products, layer_step(): jnp.einsum('nd,fd->nf', grad_low, w_down, preferred_element_type=jnp.floa...  32.9 us
    dynamic_update_slice x16, local copies, waits for them, and re-layouts, gather_group(): full = lax.dynamic_update_slice(full, piece, (x, core, 0, y, 0, 0))  26.1 us
    dot_general x1, matrix products, layer_step(): jnp.einsum('sqhd,skhd->shqk', grad_heads, value_heads, preferred_element_...  18.6 us
    unnamed x179, local copies, waits for them, and re-layouts  14.7 us
    ppermute x12, starting transfers between devices, mixed_swap(): return lax.ppermute(value, AXES, pairs)  14.6 us
  transfers between devices with their start and end apart: 53, of which 17 were waited for; matrix products, arithmetic and copies ran while one was open for 35% of the time, Pallas kernels for 0%

profile of v2, /device:TPU:0, one launch (start us, length us, event | category | flops | bytes accessed | tf_op | source)
XLA Modules:
  0.0 621.4 jit_solution(13873398510578943918)
XLA Ops:
  40.5 7.0 %collective-permute-done.13 = bf16[24,6912]{1,0:T(8,128)(2,1)S(1)} collective-permute-done((bf16[24,6912]{1,0:T(8,128)(2,1)}, bf16[24,6912]{1,0:T(8,128)(2,1)S(1)}, u32[]{:S(2)}, u32[]{:S(2)}) %collective-permute-start.13) | collective-permute-done | bytes 331808 | tf_op jit(solution)/shard_map/ppermute | solution.py:31
  50.0 7.6 %collective-permute-done.14 = bf16[24,6912]{1,0:T(8,128)(2,1)S(1)} collective-permute-done((bf16[24,6912]{1,0:T(8,128)(2,1)}, bf16[24,6912]{1,0:T(8,128)(2,1)S(1)}, u32[]{:S(2)}, u32[]{:S(2)}) %collective-permute-start.14) | collective-permute-done | bytes 331808 | tf_op jit(solution)/shard_map/ppermute | solution.py:31
  88.6 13.4 %collective-permute-done.10 = bf16[2,4,24,2432]{3,2,1,0:T(8,128)(2,1)} collective-permute-done((bf16[2,4,24,2432]{3,2,1,0:T(8,128)(2,1)}, bf16[2,4,24,2432]{3,2,1,0:T(8,128)(2,1)}, u32[]{:S(2)}, u32[]{:S(2)}) %collective-permute-start.10) | collective-permute-done | bytes 933920 | tf_op jit(solution)/shard_map/ppermute | solution.py:51
  122.8 6.1 fusion.21
  132.4 6.0 reshape.710
  138.5 6.0 copy.126
  150.1 5.9 copy.124
  161.6 6.0 copy.125
  167.5 11.3 %select_reduce_fusion = (f32[3,12,320]{2,1,0:T(8,128)S(1)}, f32[3,12,320,320]{2,3,1,0:T(8,128)}) fusion(pred[3,320,320]{1,2,0:T(8,128)(4,1)S(1)} %broadcast_compare_fusion, bf16[3,320,12,64]{1,3,2,0:T(8,128)(2,1)} %copy.124, bf16[3,320,12,64]{1,3,2,0:T(8,128)(2,1)} %copy.125), kind=kOutput, calls=%fused_computation.6 | convolution fusion | flops 482906880 | bytes 18048000 | tf_op jit(solution)/shard_map/sqhd,skhd->shqk/dot_general | solution.py:150
  178.8 10.6 %fusion = f32[3,12,320]{2,1,0:T(8,128)S(1)} fusion(f32[3,12,320,320]{2,3,1,0:T(8,128)} %get-tuple-element.103, f32[3,12,320]{2,1,0:T(8,128)S(1)} %get-tuple-element.102, pred[3,320,320]{1,2,0:T(8,128)(4,1)S(1)} %broadcast_compare_fusion), kind=kLoop, calls=%fused_computation.7 | loop fusion | flops 18420480 | bytes 15144960 | tf_op jit(solution)/shard_map/reduce_sum | solution.py:201
  189.4 12.6 %convert_bitcast_fusion = bf16[3,320,12,64]{1,3,2,0:T(8,128)(2,1)S(1)} fusion(bf16[3,320,12,64]{1,3,2,0:T(8,128)(2,1)} %copy.126, f32[3,12,320,320]{2,3,1,0:T(8,128)} %get-tuple-element.103, f32[3,12,320]{2,1,0:T(8,128)S(1)} %fusion, f32[3,12,320]{2,1,0:T(8,128)S(1)} %get-tuple-element.102, pred[3,320,320]{1,2,0:T(8,128)(4,1)S(1)} %broadcast_compare_fusion), kind=kOutput, calls=%fused_computation.79 | convolution fusion | flops 494714880 | bytes 18094080 | tf_op jit(solution)/shard_map/shqk,skhd->sqhd/dot_general | solution.py:205
  235.2 9.8 %reshape.675 = bf16[32,24,4,768]{3,2,1,0:T(4,128)(2,1)} reshape(bf16[768,3072]{1,0:T(8,128)(2,1)} %slice.241) | data formatting | bytes 9437184 | tf_op jit(solution)/shard_map/reshape | solution.py:363
  248.4 8.7 %fusion.16 = f32[960,3072]{1,0:T(8,128)S(1)} fusion(bf16[768,6912]{1,0:T(8,128)(2,1)} %bitcast.53, f32[960,768]{1,0:T(8,128)S(1)} %copy-done.6, f32[768]{0:T(1024)S(1)} %get-tuple-element.18, f32[768]{0:T(1024)S(1)} %get-tuple-element.19, f32[960]{0:T(1024)S(1)} %fusion.65, f32[960]{0:T(1024)S(1)} %broadcast_multiply_fusion.1), kind=kOutput, calls=%fused_computation.40 | convolution fusion | flops 4533534720 | bytes 19478016 | tf_op jit(solution)/shard_map/dot_general | solution.py:214
  257.2 32.9 %fusion.74 = (bf16[3072]{0:T(1024)(128)(2,1)S(1)}, bf16[960,3072]{1,0:T(8,128)(2,1)S(1)}, f32[960,3072]{1,0:T(8,128)}) fusion(f32[960,3072]{1,0:T(8,128)S(1)} %fusion.16, f32[3072]{0:T(1024)S(1)} %reshape.695, bf16[960,768]{1,0:T(8,128)(2,1)S(1)} %bitcast.318, bf16[3072,768]{1,0:T(8,128)(2,1)S(1)} %bitcast.309), kind=kOutput, calls=%fused_computation.272 | convolution fusion | flops 4748080128 | bytes 35702784 | tf_op jit(solution)/shard_map/nd,fd->nf/dot_general | solution.py:227
  290.1 9.8 %multiply_reduce_fusion.1 = (bf16[768]{0:T(1024)(128)(2,1)S(1)}, f32[960]{0:T(1024)S(1)}, bf16[768]{0:T(1024)(128)(2,1)S(1)}, f32[960,768]{1,0:T(8,128)S(1)}) fusion(f32[960,768]{1,0:T(8,128)S(1)} %copy-done.7, f32[960]{0:T(1024)S(1)} %copy-done.70, f32[960]{0:T(1024)S(1)} %copy-done.54, f32[768]{0:T(1024)S(1)} %copy-done.68, ...), kind=kOutput, calls=%fused_computation.56 | convolution fusion | flops 4535743488 | bytes 16532736 | tf_op jit(solution)/shard_map/nf,df->nd/dot_general | solution.py:232
  306.8 5.6 reshape.713
  312.4 6.4 %copy.138 = bf16[3,320,12,64]{1,3,2,0:T(8,128)(2,1)} copy(bf16[3,320,12,64]{3,2,1,0:T(8,128)(2,1)} %reshape.713) | data formatting | bytes 2949120 | tf_op jit(solution)/shard_map/reshape | solution.py:250
  318.8 18.6 %multiply_reduce_fusion = (f32[3,12,320]{2,1,0:T(8,128)S(1)}, f32[3,12,320,320]{2,3,1,0:T(8,128)}) fusion(f32[3,12,320,320]{2,3,1,0:T(8,128)} %get-tuple-element.103, f32[3,12,320]{2,1,0:T(8,128)S(1)} %copy-done.42, pred[3,320,320]{1,2,0:T(8,128)(4,1)S(1)} %copy-done.11, bf16[3,320,12,64]{1,3,2,0:T(8,128)(2,1)} %copy.138, bf16[3,320,12,64]{1,3,2,0:T(8,128)(2,1)} %copy.126), kind=kOutput, calls=%fused_computation.1 | convolution fusion | flops 490279680 | bytes 32839680 | tf_op jit(solution)/shard_map/sqhd,skhd->shqk/dot_general | solution.py:252
  337.4 12.9 %multiply_convert_fusion = bf16[3,12,320,320]{2,3,1,0:T(8,128)(2,1)S(1)} fusion(f32[3,12,320,320]{2,3,1,0:T(8,128)} %get-tuple-element.108, f32[3,12,320,320]{2,3,1,0:T(8,128)} %get-tuple-element.103, f32[3,12,320]{2,1,0:T(8,128)S(1)} %get-tuple-element.107, f32[3,12,320]{2,1,0:T(8,128)S(1)} %copy-done.42, pred[3,320,320]{1,2,0:T(8,128)(4,1)S(1)} %copy-done.11), kind=kLoop, calls=%fused_computation | loop fusion | flops 22118400 | bytes 37263360 | tf_op jit(solution)/shard_map/convert_element_type | solution.py:256
  357.4 11.2 %fusion.84 = (bf16[12,64]{1,0:T(8,128)(2,1)S(1)}, bf16[3,12,64,320]{3,2,1,0:T(8,128)(2,1)}) fusion(bf16[3,320,12,64]{1,3,2,0:T(8,128)(2,1)S(1)} %copy-done.12, f32[3,12,320,320]{2,3,1,0:T(8,128)} %get-tuple-element.103, f32[3,12,320]{2,1,0:T(8,128)S(1)} %copy-done.42, pred[3,320,320]{1,2,0:T(8,128)(4,1)S(1)} %copy-done.11), kind=kOutput, calls=%fused_computation.280 | convolution fusion | flops 488078592 | bytes 18049536 | tf_op jit(solution)/shard_map/shqk,sqhd->skhd/dot_general | solution.py:271
  397.1 5.6 convert_element_type.507
  408.3 9.8 %multiply_reduce_fusion.2 = (bf16[768]{0:T(1024)(128)(2,1)S(1)}, f32[960]{0:T(1024)S(1)}, bf16[768]{0:T(1024)(128)(2,1)S(1)}, f32[960,768]{1,0:T(8,128)}) fusion(f32[960]{0:T(1024)S(1)} %copy-done.66, f32[960]{0:T(1024)S(1)} %copy-done.64, f32[3,320,768]{2,1,0:T(8,128)S(1)} %copy-done.1, f32[768]{0:T(1024)S(1)} %copy-done.61, f32[960,768]{1,0:T(8,128)S(1)} %bitcast.293, ...), kind=kOutput, calls=%fused_computation.57 | convolution fusion | flops 3404019200 | bytes 17122560 | tf_op jit(solution)/shard_map/ne,de->nd/dot_general | solution.py:284
  418.2 7.9 %convolution_convert_fusion.2 = bf16[768,2304]{1,0:T(8,128)(2,1)} fusion(bf16[960,768]{1,0:T(8,128)(2,1)S(1)} %copy-done.35, bf16[960,2304]{0,1:T(8,128)(2,1)} %constant_dynamic-update-slice_fusion.8), kind=kOutput, calls=%fused_computation.30 | convolution fusion | flops 3399155712 | bytes 9437184 | tf_op jit(solution)/shard_map/nd,ne->de/dot_general | solution.py:281
  426.1 10.3 %convolution_convert_fusion.1 = bf16[768,3072]{1,0:T(8,128)(2,1)} fusion(bf16[960,3072]{1,0:T(8,128)(2,1)} %copy-done.75, f32[960,768]{1,0:T(8,128)} %copy-done.5, f32[768]{0:T(1024)S(1)} %copy-done.74, f32[768]{0:T(1024)S(1)} %copy-done.68, f32[960]{0:T(1024)S(1)} %copy-done.70, f32[960]{0:T(1024)S(1)} %copy-done.54), kind=kOutput, calls=%fused_computation.29 | convolution fusion | flops 4535894016 | bytes 13579776 | tf_op jit(solution)/shard_map/nd,nf->df/dot_general | solution.py:230
  442.0 8.8 %multiply_convert_fusion.5 = bf16[960,768]{1,0:T(8,128)(2,1)S(1)} fusion(f32[960,768]{1,0:T(8,128)S(1)} %copy-done.8, bf16[960,3072]{1,0:T(8,128)(2,1)} %multiply_convert_fusion.1, bf16[3072,768]{1,0:T(8,128)(2,1)} %bitcast.310, f32[768]{0:T(1024)S(1)} %copy-done.72, f32[960]{0:T(1024)S(1)} %copy-done.62), kind=kOutput, calls=%fused_computation.63 | convolution fusion | flops 4532797440 | bytes 15047424 | tf_op jit(solution)/shard_map/dot_general | solution.py:218
  472.2 8.4 %convolution_convert_fusion = bf16[3072,768]{1,0:T(8,128)(2,1)S(1)} fusion(bf16[960,3072]{1,0:T(8,128)(2,1)} %multiply_convert_fusion.1, bf16[960,768]{1,0:T(8,128)(2,1)S(1)} %copy-done.36), kind=kOutput, calls=%fused_computation.28 | convolution fusion | flops 4532207616 | bytes 12091392 | tf_op jit(solution)/shard_map/nf,nd->fd/dot_general | solution.py:225
  485.1 9.5 %reshape_reshape.22 = bf16[2,2,4,2,24,3072]{5,4,3,2,1,0:T(8,128)(2,1)} reshape(bf16[32,24,4,768]{3,2,1,0:T(4,128)(2,1)} %bitcast.296) | data formatting | bytes 9437184 | tf_op jit(solution)/shard_map/reshape;reshape | solution.py:87
  513.8 5.9 collective-permute-done.27
  541.5 8.4 %collective-permute-done.36 = bf16[2,4,24,2304]{3,2,1,0:T(8,128)(2,1)S(1)} collective-permute-done((bf16[2,4,24,2304]{3,2,1,0:T(8,128)(2,1)S(1)}, bf16[2,4,24,2304]{3,2,1,0:T(8,128)(2,1)S(1)}, u32[]{:S(2)}, u32[]{:S(2)}) %collective-permute-start.36) | collective-permute-done | bytes 884768 | tf_op jit(solution)/shard_map/ppermute | solution.py:51
  553.2 9.6 %collective-permute-done.37 = bf16[4,24,2304]{2,1,0:T(8,128)(2,1)S(1)} collective-permute-done((bf16[4,24,2304]{2,1,0:T(8,128)(2,1)S(1)}, bf16[4,24,2304]{2,1,0:T(8,128)(2,1)S(1)}, u32[]{:S(2)}, u32[]{:S(2)}) %collective-permute-start.37) | collective-permute-done | bytes 442400 | tf_op jit(solution)/shard_map/ppermute | solution.py:51
  575.4 14.7 %collective-permute-done.42 = bf16[2,4,24,3072]{3,2,1,0:T(8,128)(2,1)S(1)} collective-permute-done((bf16[2,4,24,3072]{3,2,1,0:T(8,128)(2,1)S(1)}, bf16[2,4,24,3072]{3,2,1,0:T(8,128)(2,1)S(1)}, u32[]{:S(2)}, u32[]{:S(2)}) %collective-permute-start.42) | collective-permute-done | bytes 1179680 | tf_op jit(solution)/shard_map/ppermute | solution.py:51
  607.5 7.7 %collective-permute-done.51 = bf16[24,3072]{1,0:T(8,128)(2,1)S(1)} collective-permute-done((bf16[24,3072]{1,0:T(8,128)(2,1)S(1)}, bf16[24,3072]{1,0:T(8,128)(2,1)S(1)}, u32[]{:S(2)}, u32[]{:S(2)}) %collective-permute-start.51) | collective-permute-done | bytes 147488 | tf_op jit(solution)/shard_map/ppermute | solution.py:31
  (449 shorter events, 304.2 us)
Async XLA Ops:
  8.6 25.1 %collective-permute-start.6 = (bf16[24,2432]{1,0:T(8,128)(2,1)S(1)}, bf16[24,2432]{1,0:T(8,128)(2,1)S(1)}, u32[]{:S(2)}, u32[]{:S(2)}) collective-permute-start(bf16[24,2432]{1,0:T(8,128)(2,1)S(1)} %fusion.59), channel_id=1, source_target_pairs={{0,2},{1,3},{2,0},{3,1},{4,6},{5,7},{6,4},{7,5},{8,10},{9,11},{10,... | collective-permute-start | bytes 350216 | tf_op jit(solution)/shard_map/ppermute | solution.py:31
  11.7 22.1 %collective-permute-start.7 = (bf16[24,2432]{1,0:T(8,128)(2,1)S(1)}, bf16[24,2432]{1,0:T(8,128)(2,1)S(1)}, u32[]{:S(2)}, u32[]{:S(2)}) collective-permute-start(bf16[24,2432]{1,0:T(8,128)(2,1)S(1)} %fusion.59), channel_id=1, source_target_pairs={{0,4},{1,5},{2,6},{3,7},{4,0},{5,1},{6,2},{7,3},{8,12},{9,13},{10,... | collective-permute-start | bytes 350216 | tf_op jit(solution)/shard_map/ppermute | solution.py:31
  28.2 19.4 %collective-permute-start.13 = (bf16[24,6912]{1,0:T(8,128)(2,1)}, bf16[24,6912]{1,0:T(8,128)(2,1)S(1)}, u32[]{:S(2)}, u32[]{:S(2)}) collective-permute-start(bf16[24,6912]{1,0:T(8,128)(2,1)} %slice_dynamic-update-slice_fusion.2), channel_id=1, source_target_pairs={{0,2},{1,3},{2,0},{3,1},{4,6},{5,7},{6,4},{7,5},{8,10},{9,11},{10,... | collective-permute-start | bytes 995336 | tf_op jit(solution)/shard_map/ppermute | solution.py:31
  29.1 28.5 %collective-permute-start.14 = (bf16[24,6912]{1,0:T(8,128)(2,1)}, bf16[24,6912]{1,0:T(8,128)(2,1)S(1)}, u32[]{:S(2)}, u32[]{:S(2)}) collective-permute-start(bf16[24,6912]{1,0:T(8,128)(2,1)} %slice_dynamic-update-slice_fusion.2), channel_id=1, source_target_pairs={{0,4},{1,5},{2,6},{3,7},{4,0},{5,1},{6,2},{7,3},{8,12},{9,13},{10,... | collective-permute-start | bytes 995336 | tf_op jit(solution)/shard_map/ppermute | solution.py:31
  33.7 26.5 %collective-permute-start.15 = (bf16[24,6912]{1,0:T(8,128)(2,1)}, bf16[24,6912]{1,0:T(8,128)(2,1)S(1)}, u32[]{:S(2)}, u32[]{:S(2)}) collective-permute-start(bf16[24,6912]{1,0:T(8,128)(2,1)} %slice_dynamic-update-slice_fusion.2), channel_id=1, source_target_pairs={{0,6},{1,7},{2,4},{3,5},{4,2},{5,3},{6,0},{7,1},{8,14},{9,15},{10,... | collective-permute-start | bytes 995336 | tf_op jit(solution)/shard_map/ppermute | solution.py:31
  33.8 28.3 %collective-permute-start.5 = (bf16[3,80,768]{2,1,0:T(8,128)(2,1)}, bf16[3,80,768]{2,1,0:T(8,128)(2,1)S(1)}, u32[]{:S(2)}, u32[]{:S(2)}) collective-permute-start(bf16[3,80,768]{2,1,0:T(8,128)(2,1)} %get-tuple-element.80), channel_id=1, source_target_pairs={{0,24},{1,25},{2,26},{3,27},{4,28},{5,29},{6,30},{7,31},{8,16},{9,... | collective-permute-start | bytes 1105928 | tf_op jit(solution)/shard_map/ppermute | solution.py:31
  36.0 34.0 %collective-permute-start.4 = (bf16[3,80,768]{2,1,0:T(8,128)(2,1)}, bf16[3,80,768]{2,1,0:T(8,128)(2,1)S(1)}, u32[]{:S(2)}, u32[]{:S(2)}) collective-permute-start(bf16[3,80,768]{2,1,0:T(8,128)(2,1)} %get-tuple-element.81), channel_id=1, source_target_pairs={{0,16},{1,17},{2,18},{3,19},{4,20},{5,21},{6,22},{7,23},{8,24},{9,... | collective-permute-start | bytes 1105928 | tf_op jit(solution)/shard_map/ppermute | solution.py:31
  48.3 23.0 %collective-permute-start.3 = (bf16[3,80,768]{2,1,0:T(8,128)(2,1)}, bf16[3,80,768]{2,1,0:T(8,128)(2,1)S(1)}, u32[]{:S(2)}, u32[]{:S(2)}) collective-permute-start(bf16[3,80,768]{2,1,0:T(8,128)(2,1)} %get-tuple-element.79), channel_id=1, source_target_pairs={{0,8},{1,9},{2,10},{3,11},{4,12},{5,13},{6,14},{7,15},{8,0},{9,1},... | collective-permute-start | bytes 1105928 | tf_op jit(solution)/shard_map/ppermute | solution.py:31
  60.2 16.6 %collective-permute-start.24 = (bf16[3,80,768]{2,1,0:T(8,128)(2,1)S(1)}, bf16[3,80,768]{2,1,0:T(8,128)(2,1)S(1)}, u32[]{:S(2)}, u32[]{:S(2)}) collective-permute-start(bf16[3,80,768]{2,1,0:T(8,128)(2,1)S(1)} %copy-done.45), channel_id=1, source_target_pairs={{0,16},{1,17},{2,18},{3,19},{4,20},{5,21},{6,22},{7,23},{8,24},{9,... | collective-permute-start | bytes 1105928 | tf_op jit(solution)/shard_map/ppermute | solution.py:31
  62.1 14.7 %collective-permute-start.23 = (bf16[3,80,768]{2,1,0:T(8,128)(2,1)S(1)}, bf16[3,80,768]{2,1,0:T(8,128)(2,1)S(1)}, u32[]{:S(2)}, u32[]{:S(2)}) collective-permute-start(bf16[3,80,768]{2,1,0:T(8,128)(2,1)S(1)} %copy-done.44), channel_id=1, source_target_pairs={{0,8},{1,9},{2,10},{3,11},{4,12},{5,13},{6,14},{7,15},{8,0},{9,1},... | collective-permute-start | bytes 1105928 | tf_op jit(solution)/shard_map/ppermute | solution.py:31
  71.3 37.7 %collective-permute-start.16 = (bf16[4,24,6912]{2,1,0:T(8,128)(2,1)}, bf16[4,24,6912]{2,1,0:T(8,128)(2,1)}, u32[]{:S(2)}, u32[]{:S(2)}) collective-permute-start(bf16[4,24,6912]{2,1,0:T(8,128)(2,1)} %bitcast_dynamic-update-slice_fusion.4), channel_id=1, source_target_pairs={{0,16},{1,17},{2,18},{3,19},{4,20},{5,21},{6,22},{7,23},{8,9},{9,8... | collective-permute-start | bytes 3981320 | tf_op jit(solution)/shard_map/ppermute | solution.py:51
  83.0 18.9 %collective-permute-start.10 = (bf16[2,4,24,2432]{3,2,1,0:T(8,128)(2,1)}, bf16[2,4,24,2432]{3,2,1,0:T(8,128)(2,1)}, u32[]{:S(2)}, u32[]{:S(2)}) collective-permute-start(bf16[2,4,24,2432]{3,2,1,0:T(8,128)(2,1)} %pad_maximum_fusion.4), channel_id=1, source_target_pairs={{0,1},{1,0},{2,3},{3,2},{4,5},{5,4},{6,7},{7,6},{8,24},{9,25},{10,... | collective-permute-start | bytes 2801672 | tf_op jit(solution)/shard_map/ppermute | solution.py:51
  87.6 19.8 %collective-permute-start.11 = (bf16[2,4,24,2432]{3,2,1,0:T(8,128)(2,1)}, bf16[2,4,24,2432]{3,2,1,0:T(8,128)(2,1)S(1)}, u32[]{:S(2)}, u32[]{:S(2)}) collective-permute-start(bf16[2,4,24,2432]{3,2,1,0:T(8,128)(2,1)} %pad_maximum_fusion.4), channel_id=1, source_target_pairs={{0,8},{1,9},{2,10},{3,11},{4,12},{5,13},{6,14},{7,15},{8,0},{9,1},... | collective-permute-start | bytes 2801672 | tf_op jit(solution)/shard_map/ppermute | solution.py:31
  112.5 99.8 %collective-permute-start.17 = (bf16[2,4,24,6912]{3,2,1,0:T(8,128)(2,1)}, bf16[2,4,24,6912]{3,2,1,0:T(8,128)(2,1)}, u32[]{:S(2)}, u32[]{:S(2)}) collective-permute-start(bf16[2,4,24,6912]{3,2,1,0:T(8,128)(2,1)} %pad_maximum_fusion), channel_id=1, source_target_pairs={{0,1},{1,0},{2,3},{3,2},{4,5},{5,4},{6,7},{7,6},{8,24},{9,25},{10,... | collective-permute-start | bytes 7962632 | tf_op jit(solution)/shard_map/ppermute | solution.py:51
  114.0 103.9 %collective-permute-start.18 = (bf16[2,4,24,6912]{3,2,1,0:T(8,128)(2,1)}, bf16[2,4,24,6912]{3,2,1,0:T(8,128)(2,1)}, u32[]{:S(2)}, u32[]{:S(2)}) collective-permute-start(bf16[2,4,24,6912]{3,2,1,0:T(8,128)(2,1)} %pad_maximum_fusion), channel_id=1, source_target_pairs={{0,8},{1,9},{2,10},{3,11},{4,12},{5,13},{6,14},{7,15},{8,0},{9,1},... | collective-permute-start | bytes 7962632 | tf_op jit(solution)/shard_map/ppermute | solution.py:31
  452.1 49.8 %collective-permute-start.20 = (bf16[3,80,768]{2,1,0:T(8,128)(2,1)}, bf16[3,80,768]{2,1,0:T(8,128)(2,1)}, u32[]{:S(2)}, u32[]{:S(2)}) collective-permute-start(bf16[3,80,768]{2,1,0:T(8,128)(2,1)} %get-tuple-element.72), channel_id=1, source_target_pairs={{0,8},{1,9},{2,10},{3,11},{4,12},{5,13},{6,14},{7,15},{8,0},{9,1},... | collective-permute-start | bytes 1105928 | tf_op jit(solution)/shard_map/ppermute | solution.py:31
  452.1 52.1 %collective-permute-start.21 = (bf16[3,80,768]{2,1,0:T(8,128)(2,1)}, bf16[3,80,768]{2,1,0:T(8,128)(2,1)}, u32[]{:S(2)}, u32[]{:S(2)}) collective-permute-start(bf16[3,80,768]{2,1,0:T(8,128)(2,1)} %get-tuple-element.71), channel_id=1, source_target_pairs={{0,16},{1,17},{2,18},{3,19},{4,20},{5,21},{6,22},{7,23},{8,24},{9,... | collective-permute-start | bytes 1105928 | tf_op jit(solution)/shard_map/ppermute | solution.py:31
  453.3 52.8 %collective-permute-start.22 = (bf16[3,80,768]{2,1,0:T(8,128)(2,1)}, bf16[3,80,768]{2,1,0:T(8,128)(2,1)}, u32[]{:S(2)}, u32[]{:S(2)}) collective-permute-start(bf16[3,80,768]{2,1,0:T(8,128)(2,1)} %get-tuple-element.70), channel_id=1, source_target_pairs={{0,24},{1,25},{2,26},{3,27},{4,28},{5,29},{6,30},{7,31},{8,16},{9,... | collective-permute-start | bytes 1105928 | tf_op jit(solution)/shard_map/ppermute | solution.py:31
  464.1 47.9 %collective-permute-start.26 = (bf16[3,80,768]{2,1,0:T(8,128)(2,1)}, bf16[3,80,768]{2,1,0:T(8,128)(2,1)}, u32[]{:S(2)}, u32[]{:S(2)}) collective-permute-start(bf16[3,80,768]{2,1,0:T(8,128)(2,1)} %get-tuple-element.68), channel_id=1, source_target_pairs={{0,8},{1,9},{2,10},{3,11},{4,12},{5,13},{6,14},{7,15},{8,0},{9,1},... | collective-permute-start | bytes 1105928 | tf_op jit(solution)/shard_map/ppermute | solution.py:31
  469.1 32.1 %collective-permute-start.29 = (bf16[2,4,2,24,896]{4,3,2,1,0:T(8,128)(2,1)}, bf16[2,4,2,24,896]{4,3,2,1,0:T(8,128)(2,1)S(1)}, u32[]{:S(2)}, u32[]{:S(2)}) collective-permute-start(bf16[2,4,2,24,896]{4,3,2,1,0:T(8,128)(2,1)} %dynamic-slice_bitcast_fusion.3), channel_id=1, source_target_pairs={{0,8},{1,9},{2,10},{3,11},{4,12},{5,13},{6,14},{7,15},{8,0},{9,1},... | collective-permute-start | bytes 2064392 | tf_op jit(solution)/shard_map/ppermute | solution.py:31
  501.2 32.8 %collective-permute-start.35 = (bf16[2,4,2,24,2304]{4,3,2,1,0:T(8,128)(2,1)}, bf16[2,4,2,24,2304]{4,3,2,1,0:T(8,128)(2,1)}, u32[]{:S(2)}, u32[]{:S(2)}) collective-permute-start(bf16[2,4,2,24,2304]{4,3,2,1,0:T(8,128)(2,1)} %dynamic-slice_bitcast_fusion.2), channel_id=1, source_target_pairs={{0,8},{1,9},{2,10},{3,11},{4,12},{5,13},{6,14},{7,15},{8,0},{9,1},... | collective-permute-start | bytes 5308424 | tf_op jit(solution)/shard_map/ppermute | solution.py:31
  504.2 15.5 %collective-permute-start.27 = (bf16[3,80,768]{2,1,0:T(8,128)(2,1)S(1)}, bf16[3,80,768]{2,1,0:T(8,128)(2,1)S(1)}, u32[]{:S(2)}, u32[]{:S(2)}) collective-permute-start(bf16[3,80,768]{2,1,0:T(8,128)(2,1)S(1)} %copy-done.48), channel_id=1, source_target_pairs={{0,16},{1,17},{2,18},{3,19},{4,20},{5,21},{6,22},{7,23},{8,24},{9,... | collective-permute-start | bytes 1105928 | tf_op jit(solution)/shard_map/ppermute | solution.py:31
  506.1 19.5 %collective-permute-start.28 = (bf16[3,80,768]{2,1,0:T(8,128)(2,1)S(1)}, bf16[3,80,768]{2,1,0:T(8,128)(2,1)S(1)}, u32[]{:S(2)}, u32[]{:S(2)}) collective-permute-start(bf16[3,80,768]{2,1,0:T(8,128)(2,1)S(1)} %copy-done.47), channel_id=1, source_target_pairs={{0,24},{1,25},{2,26},{3,27},{4,28},{5,29},{6,30},{7,31},{8,16},{9,... | collective-permute-start | bytes 1105928 | tf_op jit(solution)/shard_map/ppermute | solution.py:31
  511.8 26.2 %collective-permute-start.47 = (bf16[2,4,2,24,3072]{4,3,2,1,0:T(8,128)(2,1)}, bf16[2,4,2,24,3072]{4,3,2,1,0:T(8,128)(2,1)}, u32[]{:S(2)}, u32[]{:S(2)}) collective-permute-start(bf16[2,4,2,24,3072]{4,3,2,1,0:T(8,128)(2,1)} %dynamic-slice_bitcast_fusion), channel_id=1, source_target_pairs={{0,8},{1,9},{2,10},{3,11},{4,12},{5,13},{6,14},{7,15},{8,0},{9,1},... | collective-permute-start | bytes 7077896 | tf_op jit(solution)/shard_map/ppermute | solution.py:31
  552.0 21.8 %collective-permute-start.48 = (bf16[2,4,24,3072]{3,2,1,0:T(8,128)(2,1)S(1)}, bf16[2,4,24,3072]{3,2,1,0:T(8,128)(2,1)S(1)}, u32[]{:S(2)}, u32[]{:S(2)}) collective-permute-start(bf16[2,4,24,3072]{3,2,1,0:T(8,128)(2,1)S(1)} %pad_maximum_fusion.3), channel_id=1, source_target_pairs={{0,16},{1,17},{2,18},{3,19},{4,20},{5,21},{6,22},{7,23},{8,9},{9,8... | collective-permute-start | bytes 3538952 | tf_op jit(solution)/shard_map/ppermute | solution.py:51
  567.5 22.6 %collective-permute-start.42 = (bf16[2,4,24,3072]{3,2,1,0:T(8,128)(2,1)S(1)}, bf16[2,4,24,3072]{3,2,1,0:T(8,128)(2,1)S(1)}, u32[]{:S(2)}, u32[]{:S(2)}) collective-permute-start(bf16[2,4,24,3072]{3,2,1,0:T(8,128)(2,1)S(1)} %pad_maximum_fusion.2), channel_id=1, source_target_pairs={{0,16},{1,17},{2,18},{3,19},{4,20},{5,21},{6,22},{7,23},{8,9},{9,8... | collective-permute-start | bytes 3538952 | tf_op jit(solution)/shard_map/ppermute | solution.py:51
  574.2 17.4 %collective-permute-start.49 = (bf16[4,24,3072]{2,1,0:T(8,128)(2,1)S(1)}, bf16[4,24,3072]{2,1,0:T(8,128)(2,1)S(1)}, u32[]{:S(2)}, u32[]{:S(2)}) collective-permute-start(bf16[4,24,3072]{2,1,0:T(8,128)(2,1)S(1)} %dynamic-slice_bitcast_fusion.4), channel_id=1, source_target_pairs={{0,1},{1,0},{2,3},{3,2},{4,5},{5,4},{6,7},{7,6},{8,24},{9,25},{10,... | collective-permute-start | bytes 1769480 | tf_op jit(solution)/shard_map/ppermute | solution.py:51
  593.6 21.6 %collective-permute-start.51 = (bf16[24,3072]{1,0:T(8,128)(2,1)S(1)}, bf16[24,3072]{1,0:T(8,128)(2,1)S(1)}, u32[]{:S(2)}, u32[]{:S(2)}) collective-permute-start(bf16[24,3072]{1,0:T(8,128)(2,1)S(1)} %get-tuple-element.88), channel_id=1, source_target_pairs={{0,4},{1,5},{2,6},{3,7},{4,0},{5,1},{6,2},{7,3},{8,12},{9,13},{10,... | collective-permute-start | bytes 442376 | tf_op jit(solution)/shard_map/ppermute | solution.py:31
  594.8 20.3 %collective-permute-start.50 = (bf16[24,3072]{1,0:T(8,128)(2,1)S(1)}, bf16[24,3072]{1,0:T(8,128)(2,1)S(1)}, u32[]{:S(2)}, u32[]{:S(2)}) collective-permute-start(bf16[24,3072]{1,0:T(8,128)(2,1)S(1)} %get-tuple-element.86), channel_id=1, source_target_pairs={{0,2},{1,3},{2,0},{3,1},{4,6},{5,7},{6,4},{7,5},{8,10},{9,11},{10,... | collective-permute-start | bytes 442376 | tf_op jit(solution)/shard_map/ppermute | solution.py:31
  600.7 15.4 %collective-permute-start.46 = (bf16[24,3072]{1,0:T(8,128)(2,1)S(1)}, bf16[24,3072]{1,0:T(8,128)(2,1)S(1)}, u32[]{:S(2)}, u32[]{:S(2)}) collective-permute-start(bf16[24,3072]{1,0:T(8,128)(2,1)S(1)} %get-tuple-element.90), channel_id=1, source_target_pairs={{0,6},{1,7},{2,4},{3,5},{4,2},{5,3},{6,0},{7,1},{8,14},{9,15},{10,... | collective-permute-start | bytes 442376 | tf_op jit(solution)/shard_map/ppermute | solution.py:31
  602.7 17.8 %collective-permute-start.45 = (bf16[24,3072]{1,0:T(8,128)(2,1)S(1)}, bf16[24,3072]{1,0:T(8,128)(2,1)S(1)}, u32[]{:S(2)}, u32[]{:S(2)}) collective-permute-start(bf16[24,3072]{1,0:T(8,128)(2,1)S(1)} %get-tuple-element.91), channel_id=1, source_target_pairs={{0,4},{1,5},{2,6},{3,7},{4,0},{5,1},{6,2},{7,3},{8,12},{9,13},{10,... | collective-permute-start | bytes 442376 | tf_op jit(solution)/shard_map/ppermute | solution.py:31
  603.6 16.9 %collective-permute-start.44 = (bf16[24,3072]{1,0:T(8,128)(2,1)S(1)}, bf16[24,3072]{1,0:T(8,128)(2,1)S(1)}, u32[]{:S(2)}, u32[]{:S(2)}) collective-permute-start(bf16[24,3072]{1,0:T(8,128)(2,1)S(1)} %get-tuple-element.89), channel_id=1, source_target_pairs={{0,2},{1,3},{2,0},{3,1},{4,6},{5,7},{6,4},{7,5},{8,10},{9,11},{10,... | collective-permute-start | bytes 442376 | tf_op jit(solution)/shard_map/ppermute | solution.py:31
  (107 other events, 1696.3 us)

commit v3 on v2

v3 whole, which is shorter than its diff:
```python
import jax
import jax.numpy as jnp
from jax import lax
from jax.experimental import pallas as pl
from jax.experimental.pallas import tpu as pltpu
from jax.sharding import PartitionSpec as P

HEADS = 12
EPSILON = 1e-06
AXES = ("frame", "clip")


class Grid:
    def __init__(self, frames, clips):
        self.frames = frames
        self.clips = clips
        self.sizes = {"x": frames // 2, "core": 2, "z": clips // 2, "y": 2}

    def here(self):
        frame = lax.axis_index("frame")
        clip = lax.axis_index("clip")
        return {"x": frame // 2, "core": frame % 2, "z": clip // 2, "y": clip % 2}

    def swap(self, value, **flips):
        pairs = []
        for index in range(self.frames * self.clips):
            frame, clip = divmod(index, self.clips)
            at = {"x": frame // 2, "core": frame % 2, "z": clip // 2, "y": clip % 2}
            for name, bits in flips.items():
                at[name] ^= bits
            other = (at["x"] * 2 + at["core"]) * self.clips + at["z"] * 2 + at["y"]
            pairs.append((index, other))
        return lax.ppermute(value, AXES, pairs)


def put(buffer, piece, axis, index):
    return lax.dynamic_update_index_in_dim(buffer, piece, index, axis)


def pick(value, axis, index):
    return lax.dynamic_index_in_dim(value, index, axis, keepdims=False)


def mixed_swap(grid, value, first):
    pairs = []
    for index in range(grid.frames * grid.clips):
        frame, clip = divmod(index, grid.clips)
        if frame % 2 == first:
            frame ^= 2
        else:
            clip ^= 1
        pairs.append((index, frame * grid.clips + clip))
    return lax.ppermute(value, AXES, pairs)


def cell(here, core, near, far):
    x = jnp.where(core == 0, here["x"] ^ near, here["x"] ^ far)
    y = jnp.where(core == 0, here["y"] ^ far, here["y"] ^ near)
    return x, y


def gather_group(grid, here, shard):
    count = grid.sizes["z"]
    rows, width = shard.shape
    column = jnp.zeros((count, rows, width), shard.dtype)
    for bits in range(count):
        part = grid.swap(shard, z=bits) if bits else shard
        column = put(column, part, 0, here["z"] ^ bits)
    pair = jnp.stack([column, mixed_swap(grid, column, 0)])
    other = mixed_swap(grid, pair, 1)
    halves = ((pair, other), (grid.swap(pair, core=1), grid.swap(other, core=1)))
    full = jnp.zeros((grid.sizes["x"], 2, count, 2, rows, width), shard.dtype)
    for side in range(2):
        core = here["core"] ^ side
        for far in range(2):
            for near in range(2):
                x, y = cell(here, core, near, far)
                piece = halves[side][far][near][None, None, :, None]
                full = lax.dynamic_update_slice(full, piece, (x, core, 0, y, 0, 0))
    return full.reshape(-1, width)


def scatter_group(grid, here, grad):
    sizes = grid.sizes
    count = sizes["z"]
    width = grad.shape[1]
    rows = grad.shape[0] // (grid.frames * grid.clips)
    core = here["core"]
    value = grad.reshape((sizes["x"], 2, count, 2, rows, width))
    value = pick(value, 1, core).astype(jnp.float32) + grid.swap(pick(value, 1, 1 - core), core=1).astype(jnp.float32)
    value = value.astype(jnp.bfloat16)

    def piece(near, far):
        x = jnp.where(core == 0, here["x"] ^ near, far)
        y = jnp.where(core == 0, far, here["y"] ^ near)
        return lax.dynamic_slice(value, (x, 0, y, 0, 0), (1, count, 1, rows, width))[0, :, 0]

    sent = jnp.stack([piece(1, 0), piece(1, 1)])
    kept = jnp.stack([piece(0, 0), piece(0, 1)])
    value = (kept.astype(jnp.float32) + mixed_swap(grid, sent, 0).astype(jnp.float32)).astype(jnp.bfloat16)
    own = jnp.where(core == 0, here["y"], here["x"])
    value = pick(value, 0, own).astype(jnp.float32) + mixed_swap(grid, pick(value, 0, 1 - own), 1).astype(jnp.float32)
    value = value.astype(jnp.bfloat16)
    total = pick(value, 0, here["z"]).astype(jnp.float32)
    for bits in range(1, count):
        total = total + grid.swap(pick(value, 0, here["z"] ^ bits), z=bits).astype(jnp.float32)
    return total


def to_slots(grid, here, value):
    own = value.shape[0] // grid.frames
    frame = here["x"] * 2 + here["core"]
    pieces = []
    for bits in range(grid.frames):
        piece = lax.dynamic_slice_in_dim(value, (frame ^ bits) * own, own, 0)
        if bits:
            piece = grid.swap(piece, x=bits // 2, core=bits % 2)
        pieces.append(piece)
    return jnp.concatenate(pieces, axis=1)


def from_slots(grid, here, value):
    frames = grid.frames
    own, length = value.shape[:2]
    width = length // frames
    frame = here["x"] * 2 + here["core"]
    buffer = jnp.zeros((own * frames, width) + value.shape[2:], value.dtype)
    for bits in range(frames):
        piece = value[:, bits * width : (bits + 1) * width]
        if bits:
            piece = grid.swap(piece, x=bits // 2, core=bits % 2)
        buffer = lax.dynamic_update_slice_in_dim(buffer, piece, (frame ^ bits) * own, 0)
    return buffer


ROOT_HALF = 0.7071067811865476
DENSITY = 0.3989422804014327
NT = (((1,), (1,)), ((), ()))
NN = (((1,), (0,)), ((), ()))
TN = (((0,), (0,)), ((), ()))


def dot(left, right, dims=NN):
    return lax.dot_general(left, right, dims, preferred_element_type=jnp.float32)


def normalize(values):
    center = values - jnp.mean(values, axis=-1, keepdims=True)
    spread = jnp.mean(center * center, axis=-1, keepdims=True)
    scale = lax.rsqrt(spread + EPSILON)
    return center * scale, scale


def gelu_parts(u):
    size = jnp.abs(u)
    bell = jnp.exp(-0.5 * (u * u))
    t = 1.0 / (1.0 + (0.3275911 * ROOT_HALF) * size)
    poly = t * (
        0.5 * 0.254829592
        + t * (0.5 * -0.284496736 + t * (0.5 * 1.421413741 + t * (0.5 * -1.453152027 + t * (0.5 * 1.061405429))))
    )
    tail = poly * bell
    value = jnp.maximum(u, 0.0) - size * tail
    slope = jnp.where(u > 0, 1.0 - tail, tail) + DENSITY * (u * bell)
    return value, slope


def add_rows(ref, values):
    total = jnp.sum(values, axis=0, keepdims=True)

    @pl.when(pl.program_id(0) == 0)
    def _():
        ref[...] = total

    @pl.when(pl.program_id(0) != 0)
    def _():
        ref[...] += total


def attend_kernel(x_ref, w_ref, vec_ref, seg_ref, code_ref, h_ref, qkv_ref, o_ref, p_ref):
    model = x_ref.shape[-1]
    head = model // HEADS
    n, _ = normalize(x_ref[0].astype(jnp.float32))
    low = (n * vec_ref[0:1] + vec_ref[1:2]).astype(jnp.bfloat16)
    h_ref[0] = low
    q = dot(low, w_ref[:, :model]) + vec_ref[2:3]
    qkv_ref[0, :, :model] = q.astype(jnp.bfloat16) * jnp.bfloat16(head**-0.5)
    qkv_ref[0, :, model : 2 * model] = dot(low, w_ref[:, model : 2 * model]).astype(jnp.bfloat16)
    v = dot(low, w_ref[:, 2 * model : 3 * model]) + vec_ref[3:4]
    qkv_ref[0, :, 2 * model :] = v.astype(jnp.bfloat16)
    bias = jnp.where(seg_ref[0] == code_ref[0], 0.0, -1e30)
    for i in range(HEADS):
        at = slice(i * head, (i + 1) * head)
        k_at = slice(model + i * head, model + (i + 1) * head)
        v_at = slice(2 * model + i * head, 2 * model + (i + 1) * head)
        s = dot(qkv_ref[0, :, at], qkv_ref[0, :, k_at], NT) + bias
        e = jnp.exp(s - jnp.max(s, axis=-1, keepdims=True))
        p = (e * (1.0 / jnp.sum(e, axis=-1, keepdims=True))).astype(jnp.bfloat16)
        p_ref[0, i] = p
        o_ref[0, :, at] = dot(p, qkv_ref[0, :, v_at]).astype(jnp.bfloat16)


def up_kernel(x_ref, o_ref, wo_ref, u0, u1, u2, u3, vec_ref, ub_ref, x2_ref, h2_ref, a_ref, gp_ref):
    x2 = x_ref[0].astype(jnp.float32) + (dot(o_ref[0], wo_ref[...]) + vec_ref[4:5])
    x2_ref[0] = x2
    n, _ = normalize(x2)
    low = (n * vec_ref[5:6] + vec_ref[6:7]).astype(jnp.bfloat16)
    h2_ref[0] = low
    width = wo_ref.shape[1]
    for j, w in enumerate((u0, u1, u2, u3)):
        at = slice(j * width, (j + 1) * width)
        u = dot(low, w[...]) + ub_ref[:, at]
        value, slope = gelu_parts(u)
        a_ref[0, :, at] = value.astype(jnp.bfloat16)
        gp_ref[0, :, at] = slope.astype(jnp.bfloat16)


def down_kernel(x2_ref, a_ref, gp_ref, wd_ref, cot_ref, keep_ref, vec_ref, out_ref, gm_ref, gu_ref, gdb_ref, gub_ref):
    keep = keep_ref[0]
    y = x2_ref[0] + (dot(a_ref[0], wd_ref[...]) + vec_ref[7:8])
    out_ref[0] = (keep * y).astype(jnp.bfloat16)
    gy = keep * cot_ref[0].astype(jnp.float32)
    gm = gy.astype(jnp.bfloat16)
    gm_ref[0] = gm
    add_rows(gdb_ref, gy)
    model = gm.shape[1]
    for j in range(a_ref.shape[2] // model):
        at = slice(j * model, (j + 1) * model)
        ga = dot(gm, wd_ref[at, :], NT)
        gu = (ga * gp_ref[0, :, at].astype(jnp.float32)).astype(jnp.bfloat16)
        gu_ref[0, :, at] = gu
        add_rows(gub_ref.at[:, at], gu.astype(jnp.float32))


def norm_back(grad, n, scale, gain):
    gn = grad * gain
    mean = jnp.mean(gn, axis=-1, keepdims=True)
    cross = jnp.mean(gn * n, axis=-1, keepdims=True)
    return (gn - mean - n * cross) * scale


def middle_kernel(gu_ref, u0, u1, u2, u3, wo_ref, x2_ref, gm_ref, vec_ref, gx_ref, ga_ref, go_ref, gg_ref, gb_ref, gob_ref):
    width = wo_ref.shape[1]
    gh = None
    for j, w in enumerate((u0, u1, u2, u3)):
        part = dot(gu_ref[0, :, j * width : (j + 1) * width], w[...], NT)
        gh = part if gh is None else gh + part
    n, scale = normalize(x2_ref[0])
    add_rows(gg_ref, gh * n)
    add_rows(gb_ref, gh)
    gx = gm_ref[0].astype(jnp.float32) + norm_back(gh, n, scale, vec_ref[5:6])
    gx_ref[0] = gx
    low = gx.astype(jnp.bfloat16)
    ga_ref[0] = low
    add_rows(gob_ref, low.astype(jnp.float32))
    go_ref[0] = dot(low, wo_ref[...], NT).astype(jnp.bfloat16)


def attend_back_kernel(qkv_ref, go_ref, p_ref, g_ref, gqb_ref, gvb_ref):
    model = go_ref.shape[-1]
    head = model // HEADS
    for i in range(HEADS):
        at = slice(i * head, (i + 1) * head)
        k_at = slice(model + i * head, model + (i + 1) * head)
        v_at = slice(2 * model + i * head, 2 * model + (i + 1) * head)
        go = go_ref[0, :, at]
        p = p_ref[0, i]
        dp = dot(go, qkv_ref[0, :, v_at], NT)
        pf = p.astype(jnp.float32)
        delta = jnp.sum(pf * dp, axis=-1, keepdims=True)
        ds = (pf * (dp - delta)).astype(jnp.bfloat16)
        g_ref[0, :, at] = (dot(ds, qkv_ref[0, :, k_at]) * head**-0.5).astype(jnp.bfloat16)
        g_ref[0, :, k_at] = dot(ds, qkv_ref[0, :, at], TN).astype(jnp.bfloat16)
        g_ref[0, :, v_at] = dot(p, go, TN).astype(jnp.bfloat16)
    add_rows(gqb_ref, g_ref[0, :, :model].astype(jnp.float32))
    add_rows(gvb_ref, g_ref[0, :, 2 * model :].astype(jnp.float32))


def input_kernel(g_ref, w_ref, x_ref, gx_ref, vec_ref, out_ref, gg_ref, gb_ref):
    model = x_ref.shape[-1]
    gh = dot(g_ref[0], w_ref[:, : 3 * model], NT)
    n, scale = normalize(x_ref[0].astype(jnp.float32))
    add_rows(gg_ref, gh * n)
    add_rows(gb_ref, gh)
    out_ref[0] = (gx_ref[0] + norm_back(gh, n, scale, vec_ref[0:1])).astype(jnp.bfloat16)


def call(kernel, inputs, outputs, slots, flops, limit=56):
    specs = []
    for array, kind in inputs:
        if kind == "slot":
            rest = array.shape[1:]
            specs.append(pl.BlockSpec((1,) + rest, lambda i, n=len(rest): (i,) + (0,) * n))
        elif kind == "whole":
            specs.append(pl.BlockSpec(array.shape, lambda i, n=array.ndim: (0,) * n))
        else:
            rows = array.shape[0]
            specs.append(pl.BlockSpec((rows, rows), lambda i, j=kind: (0, j)))
    shapes = []
    places = []
    for shape, dtype in outputs:
        shapes.append(jax.ShapeDtypeStruct(shape, dtype))
        if len(shape) > 2:
            places.append(pl.BlockSpec((1,) + shape[1:], lambda i, n=len(shape) - 1: (i,) + (0,) * n))
        else:
            places.append(pl.BlockSpec(shape, lambda i: (0, 0)))
    moved = sum(a.size * a.dtype.itemsize for a, k in inputs if isinstance(k, str))
    moved += sum(s.size * s.dtype.itemsize for s in shapes)
    return pl.pallas_call(
        kernel,
        grid=(slots,),
        in_specs=specs,
        out_specs=places,
        out_shape=shapes,
        compiler_params=pltpu.CompilerParams(vmem_limit_bytes=limit * 1024 * 1024),
        cost_estimate=pl.CostEstimate(flops=flops, bytes_accessed=moved, transcendentals=0),
    )(*[a for a, _ in inputs])


def tn_grad(left, right):
    return jnp.einsum(
        "snd,sne->de", left, right, preferred_element_type=jnp.float32
    ).astype(jnp.bfloat16)


def layer(x, cot, segment, code, keep, mixed, upper, down, vec, up_bias):
    slots, length, model = x.shape
    rows = slots * length
    hidden = down.shape[0]
    bf, f32 = jnp.bfloat16, jnp.float32
    seg = segment[:, :, None]
    codes = code[:, None, :]
    kept = keep[:, :, None]
    full = (slots, length, model)
    scores = 2 * rows * length * model
    h1, qkv, o, p = call(
        attend_kernel,
        [(x, "slot"), (mixed, "whole"), (vec, "whole"), (seg, "slot"), (codes, "slot")],
        [(full, bf), ((slots, length, 3 * model), bf), (full, bf), ((slots, HEADS, length, length), bf)],
        slots,
        6 * rows * model * model + 8 * scores,
    )
    up_cols = [(upper, j) for j in range(1, 1 + hidden // model)]
    x2, h2, a, gp = call(
        up_kernel,
        [(x, "slot"), (o, "slot"), (upper, 0)] + up_cols + [(vec, "whole"), (up_bias, "whole")],
        [(full, f32), (full, bf), ((slots, length, hidden), bf), ((slots, length, hidden), bf)],
        slots,
        2 * rows * model * (model + 2 * hidden),
    )
    out, gm, gu, gdb, gub = call(
        down_kernel,
        [(x2, "slot"), (a, "slot"), (gp, "slot"), (down, "whole"), (cot, "slot"), (kept, "slot"), (vec, "whole")],
        [(full, bf), (full, bf), ((slots, length, hidden), bf), ((1, model), f32), ((1, hidden), f32)],
        slots,
        4 * rows * model * hidden,
    )
    g_down = tn_grad(a, gm)
    gx, ga, go, gmg, gmb, gob = call(
        middle_kernel,
        [(gu, "slot")] + up_cols + [(upper, 0), (x2, "slot"), (gm, "slot"), (vec, "whole")],
        [(full, f32), (full, bf), (full, bf)] + [((1, model), f32)] * 3,
        slots,
        2 * rows * model * (model + hidden),
    )
    g_up = tn_grad(h2, gu)
    g_mix, gqb, gvb = call(
        attend_back_kernel,
        [(qkv, "slot"), (go, "slot"), (p, "slot")],
        [((slots, length, 3 * model), bf)] + [((1, model), f32)] * 2,
        slots,
        16 * scores,
    )
    g_qkv = tn_grad(h1, g_mix)
    in_grad, gag, gab = call(
        input_kernel,
        [(g_mix, "slot"), (mixed, "whole"), (x, "slot"), (gx, "slot"), (vec, "whole")],
        [(full, bf)] + [((1, model), f32)] * 2,
        slots,
        6 * rows * model * model,
    )
    g_out = tn_grad(o, ga)
    return out, in_grad, g_down, g_up, g_qkv, g_out, (gag, gab, gqb, gvb, gob, gmg, gmb, gdb), gub


def body(
    grid,
    tokens,
    cotangent,
    frame_count,
    image_group,
    keep_mask,
    attn_norm_gain,
    attn_norm_bias,
    w_qkv,
    query_bias,
    value_bias,
    w_out,
    out_bias,
    mlp_norm_gain,
    mlp_norm_bias,
    w_up,
    up_bias,
    w_down,
    down_bias,
):
    here = grid.here()
    frames_here = image_group.shape[1]
    block_width = keep_mask.shape[1] // frames_here
    frame_index = lax.axis_index("frame") * frames_here + jnp.arange(frames_here, dtype=jnp.int32)
    segment = jnp.where(frame_index[None, :] < frame_count[:, None], 0, 1 + image_group)
    token_segment = jnp.repeat(segment, block_width, axis=1)
    tags = to_slots(grid, here, token_segment * 2 + keep_mask)
    token_segment = tags // 2
    keep_slots = tags % 2
    key_code = jnp.where(keep_slots == 1, token_segment, -1)
    kept_rows = keep_slots.astype(jnp.float32)

    rows = w_out.shape[0]
    ratio = up_bias.shape[0] // rows
    small = jnp.stack(
        [attn_norm_gain, attn_norm_bias, query_bias, value_bias, out_bias, mlp_norm_gain, mlp_norm_bias, down_bias],
        axis=1,
    )
    small = jnp.concatenate([small, up_bias.reshape(rows, ratio)], axis=1)
    small = jnp.pad(small, ((0, 0), (0, 128 - small.shape[1])))
    token_rows = to_slots(grid, here, tokens)

    mixed = gather_group(grid, here, jnp.concatenate([w_qkv, small], axis=1))
    upper = gather_group(grid, here, jnp.concatenate([w_out, w_up], axis=1))
    down = gather_group(grid, here, w_down)
    cotangent_rows = to_slots(grid, here, cotangent)
    vec = mixed[:, w_qkv.shape[1] :].astype(jnp.float32).T
    up_bias_row = vec[8 : 8 + ratio].T.reshape(1, -1)
    output_rows, input_rows, g_down, g_up, g_qkv, g_out, sums, g_up_bias = layer(
        token_rows, cotangent_rows, token_segment, key_code, kept_rows, mixed, upper, down, vec[:8], up_bias_row
    )
    output = from_slots(grid, here, output_rows)
    g_down = scatter_group(grid, here, g_down)
    g_up = scatter_group(grid, here, g_up)
    g_qkv = scatter_group(grid, here, g_qkv)
    input_grad = from_slots(grid, here, input_rows).astype(jnp.float32)
    model = w_out.shape[1]
    pack = jnp.concatenate(list(sums) + [g_up_bias.reshape(-1, ratio).T], axis=0)
    pack = jnp.pad(pack, ((0, 128 - pack.shape[0]), (0, 0))).T.astype(jnp.bfloat16)
    last = scatter_group(grid, here, jnp.concatenate([g_out, pack], axis=1))
    v = [last[:, model + i] for i in range(8)]
    return (
        output, input_grad, v[0], v[1], g_qkv, v[2], v[3], last[:, :model], v[4], v[5], v[6],
        g_up, last[:, model + 8 : model + 8 + ratio].reshape(-1), g_down, v[7],
    )


def solution(mesh):
    grid = Grid(mesh.shape["frame"], mesh.shape["clip"])

    def run(*arguments):
        return body(grid, *arguments)

    placed = (
        P("clip", "frame", None),
        P("clip", "frame", None),
        P("clip"),
        P("clip", "frame"),
        P("clip", "frame"),
        P(("frame", "clip")),
        P(("frame", "clip")),
        P(("frame", "clip"), None),
        P(("frame", "clip")),
        P(("frame", "clip")),
        P(("frame", "clip"), None),
        P(("frame", "clip")),
        P(("frame", "clip")),
        P(("frame", "clip")),
        P(("frame", "clip"), None),
        P(("frame", "clip")),
        P(("frame", "clip"), None),
        P(("frame", "clip")),
    )
    return jax.shard_map(
        run,
        mesh=mesh,
        in_specs=placed,
        out_specs=(
            P("clip", "frame", None),
            P("clip", "frame", None),
            P(("frame", "clip")),
            P(("frame", "clip")),
            P(("frame", "clip"), None),
            P(("frame", "clip")),
            P(("frame", "clip")),
            P(("frame", "clip"), None),
            P(("frame", "clip")),
            P(("frame", "clip")),
            P(("frame", "clip")),
            P(("frame", "clip"), None),
            P(("frame", "clip")),
            P(("frame", "clip"), None),
            P(("frame", "clip")),
        ),
        check_vma=False,
    )
```

time: 633 us -> 458 us (0.72)
  matrix products: 175 us -> 21.6 us
  local copies, waits for them, and re-layouts: 209 us -> 60.2 us
  Pallas kernels: 0 us -> 119 us
  other arithmetic: 72.8 us -> 22.6 us
  waiting for transfers between devices: 102 us -> 151 us
  starting transfers between devices: 61.2 us -> 74.8 us
    dot_general x18 -> x4, matrix products: 175 us -> 21.6 us  [tn_grad(): jnp.einsum('snd,sne->de', left, right, preferred_element_type=jnp.float32)]
    pallas_call x0 -> x6, Pallas kernels: none -> 119 us  [call(): pl.pallas_call(kernel, grid=(slots,), in_specs=specs, out_specs=places, o...]
    another operation x17 -> x2, local copies, waits for them, and re-layouts: 45.6 us -> 0.2 us  [the longest x2 12 us: layer_step(): value_heads = value_all.reshape(slot_count, key_length, HEADS, head_dim)]
    convert_element_type x9 -> x1, local copies, waits for them, and re-layouts: 35.4 us -> 0.02 us  [body(): jnp.pad(pack, ((0, 128 - pack.shape[0]), (0, 0))).T.astype(jnp.bfloat16)]
    convert_element_type x9 -> x1, other arithmetic: 33.6 us -> 1.87 us  [body(): input_grad = from_slots(grid, here, input_rows).astype(jnp.float32)]
    reshape x9 -> x4, local copies, waits for them, and re-layouts: 30.9 us -> 2.02 us  [the longest x1 0.86 us: body(): up_bias_row = vec[8:8 + ratio].T.reshape(1, -1)]
    ppermute x41 -> x46, waiting for transfers between devices: 44.2 us -> 72.1 us  [swap(): return lax.ppermute(value, AXES, pairs)]
    ppermute x12 -> x14, waiting for transfers between devices: 57.7 us -> 78.7 us  [mixed_swap(): return lax.ppermute(value, AXES, pairs)]
  transfers between devices with their start and end apart: 53 -> 60, of which waited for: 17 -> 24; matrix products, arithmetic and copies ran while one was open for 35% -> 18% of each run, Pallas kernels for 0% -> 17%
where the time goes in v3:
time: 458 us; the launch traced here: 451 us
  waiting for transfers between devices  151 us (33%)
  Pallas kernels  119 us (26%)
  starting transfers between devices  74.8 us (16%)
  local copies, waits for them, and re-layouts  60.2 us (13%)
  other arithmetic  22.6 us (5%)
  matrix products  21.6 us (5%)
    pallas_call x6, Pallas kernels, call(): pl.pallas_call(kernel, grid=(slots,), in_specs=specs, out_specs=places, o...  119 us
    ppermute x14, waiting for transfers between devices, mixed_swap(): return lax.ppermute(value, AXES, pairs)  78.7 us
    ppermute x46, waiting for transfers between devices, swap(): return lax.ppermute(value, AXES, pairs)  72.1 us
    ppermute x46, starting transfers between devices, swap(): return lax.ppermute(value, AXES, pairs)  55.5 us
    dot_general x4, matrix products, tn_grad(): jnp.einsum('snd,sne->de', left, right, preferred_element_type=jnp.float32)  21.6 us
    ppermute x14, starting transfers between devices, mixed_swap(): return lax.ppermute(value, AXES, pairs)  19.3 us
    dynamic_update_slice x24, local copies, waits for them, and re-layouts, gather_group(): full = lax.dynamic_update_slice(full, piece, (x, core, 0, y, 0, 0))  14.1 us
  transfers between devices with their start and end apart: 60, of which 24 were waited for; matrix products, arithmetic and copies ran while one was open for 18% of the time, Pallas kernels for 17%

profile of v3, /device:TPU:0, one launch (start us, length us, event | category | flops | bytes accessed | tf_op | source)
XLA Modules:
  0.0 451.3 jit_solution(10112313351188617836)
XLA Ops:
  28.7 3.6 collective-permute-start.4
  40.3 6.3 %collective-permute-done.4 = bf16[24,2432]{1,0:T(8,128)(2,1)} collective-permute-done((bf16[24,2432]{1,0:T(8,128)(2,1)}, bf16[24,2432]{1,0:T(8,128)(2,1)}, u32[]{:S(2)}, u32[]{:S(2)}) %collective-permute-start.4) | collective-permute-done | bytes 116768 | tf_op jit(solution)/shard_map/ppermute | solution.py:33
  54.8 6.3 %collective-permute-done.21 = bf16[96,768]{1,0:T(8,128)(2,1)S(1)} collective-permute-done((bf16[96,768]{1,0:T(8,128)(2,1)S(1)}, bf16[96,768]{1,0:T(8,128)(2,1)S(1)}, u32[]{:S(2)}, u32[]{:S(2)}) %collective-permute-start.21) | collective-permute-done | bytes 147488 | tf_op jit(solution)/shard_map/ppermute | solution.py:33
  69.0 3.6 collective-permute-done.1
  82.9 5.4 %collective-permute-done.28 = bf16[3,80,768]{2,1,0:T(8,128)(2,1)S(1)} collective-permute-done((bf16[3,80,768]{2,1,0:T(8,128)(2,1)S(1)}, bf16[3,80,768]{2,1,0:T(8,128)(2,1)S(1)}, u32[]{:S(2)}, u32[]{:S(2)}) %collective-permute-start.28) | collective-permute-done | bytes 368672 | tf_op jit(solution)/shard_map/ppermute | solution.py:33
  88.4 7.1 %collective-permute-done.29 = bf16[3,80,768]{2,1,0:T(8,128)(2,1)S(1)} collective-permute-done((bf16[3,80,768]{2,1,0:T(8,128)(2,1)S(1)}, bf16[3,80,768]{2,1,0:T(8,128)(2,1)S(1)}, u32[]{:S(2)}, u32[]{:S(2)}) %collective-permute-start.29) | collective-permute-done | bytes 368672 | tf_op jit(solution)/shard_map/ppermute | solution.py:33
  96.7 5.2 %collective-permute-done.6 = bf16[4,24,2432]{2,1,0:T(8,128)(2,1)S(1)} collective-permute-done((bf16[4,24,2432]{2,1,0:T(8,128)(2,1)S(1)}, bf16[4,24,2432]{2,1,0:T(8,128)(2,1)S(1)}, u32[]{:S(2)}, u32[]{:S(2)}) %collective-permute-start.6) | collective-permute-done | bytes 466976 | tf_op jit(solution)/shard_map/ppermute | solution.py:53
  103.7 10.9 %collective-permute-done.23 = bf16[4,96,768]{2,1,0:T(8,128)(2,1)S(1)} collective-permute-done((bf16[4,96,768]{2,1,0:T(8,128)(2,1)S(1)}, bf16[4,96,768]{2,1,0:T(8,128)(2,1)S(1)}, u32[]{:S(2)}, u32[]{:S(2)}) %collective-permute-start.23) | collective-permute-done | bytes 589856 | tf_op jit(solution)/shard_map/ppermute | solution.py:53
  116.4 14.0 %collective-permute-done.16 = bf16[4,24,3840]{2,1,0:T(8,128)(2,1)S(1)} collective-permute-done((bf16[4,24,3840]{2,1,0:T(8,128)(2,1)S(1)}, bf16[4,24,3840]{2,1,0:T(8,128)(2,1)S(1)}, u32[]{:S(2)}, u32[]{:S(2)}) %collective-permute-start.16) | collective-permute-done | bytes 737312 | tf_op jit(solution)/shard_map/ppermute | solution.py:53
  133.9 4.0 collective-permute-start.26
  140.2 9.8 %collective-permute-done.17 = bf16[2,4,24,3840]{3,2,1,0:T(8,128)(2,1)S(1)} collective-permute-done((bf16[2,4,24,3840]{3,2,1,0:T(8,128)(2,1)S(1)}, bf16[2,4,24,3840]{3,2,1,0:T(8,128)(2,1)S(1)}, u32[]{:S(2)}, u32[]{:S(2)}) %collective-permute-start.17) | collective-permute-done | bytes 1474592 | tf_op jit(solution)/shard_map/ppermute | solution.py:53
  150.0 3.4 collective-permute-start.19
  160.9 24.9 %shard_map.289 = (bf16[3,320,768]{2,1,0:T(8,128)(2,1)}, bf16[3,320,2304]{2,1,0:T(8,128)(2,1)}, bf16[3,320,768]{2,1,0:T(8,128)(2,1)}, bf16[3,12,320,320]{3,2,1,0:T(8,128)(2,1)}) custom-call(bf16[3,320,768]{2,1,0:T(8,128)(2,1)} %pad_maximum_fusion.x_ref, bf16[768,2432]{1,0:T(8,128)(2,1)} %bitcast.311, f32[8,768]{1,0:T(8,128)} %slice.163.vec_ref, ...), custom_call_target="tpu_custom_call" | custom-call | flops 7172259840 | bytes 19987968 | tf_op jit(solution)/shard_map/pallas_call | solution.py:309
  191.6 21.5 %shard_map.290 = (f32[3,320,768]{2,1,0:T(8,128)}, bf16[3,320,768]{2,1,0:T(8,128)(2,1)}, bf16[3,320,3072]{2,1,0:T(8,128)(2,1)}, bf16[3,320,3072]{2,1,0:T(8,128)(2,1)}) custom-call(bf16[3,320,768]{2,1,0:T(8,128)(2,1)} %pad_maximum_fusion.x_ref, bf16[3,320,768]{2,1,0:T(8,128)(2,1)} %get-tuple-element.40.o_ref, bf16[768,3840]{1,0:T(8,128)(2,1)} %bitcast.59.wo_ref.u0.u1.u2.u3, ...), custom_call_target="tpu_custom_call" | custom-call | flops 10192158720 | bytes 19206144 | tf_op jit(solution)/shard_map/pallas_call | solution.py:309
  213.1 22.8 %shard_map.291 = (bf16[3,320,768]{2,1,0:T(8,128)(2,1)}, bf16[3,320,768]{2,1,0:T(8,128)(2,1)}, bf16[3,320,3072]{2,1,0:T(8,128)(2,1)}, f32[1,768]{1,0:T(1,128)}, f32[1,3072]{1,0:T(1,128)}) custom-call(f32[3,320,768]{2,1,0:T(8,128)} %get-tuple-element.41.x2_ref, bf16[3,320,3072]{2,1,0:T(8,128)(2,1)} %get-tuple-element.42.a_ref, ...), custom_call_target="tpu_custom_call" | custom-call | flops 9059696640 | bytes 29829888 | tf_op jit(solution)/shard_map/pallas_call | solution.py:309
  235.9 6.9 %bitcast_convert_fusion = bf16[3072,768]{1,0:T(8,128)(2,1)S(1)} fusion(bf16[3,320,3072]{2,1,0:T(8,128)(2,1)S(1)} %copy-done.24, bf16[3,320,768]{2,1,0:T(8,128)(2,1)} %get-tuple-element.47.gm_ref), kind=kOutput, calls=%fused_computation | convolution fusion | flops 4532207616 | bytes 12091392 | tf_op jit(solution)/shard_map/snd,sne->de/dot_general | solution.py:321
  246.3 16.0 %shard_map.292 = (f32[3,320,768]{2,1,0:T(8,128)}, bf16[3,320,768]{2,1,0:T(8,128)(2,1)}, bf16[3,320,768]{2,1,0:T(8,128)(2,1)}, f32[1,768]{1,0:T(1,128)}, f32[1,768]{1,0:T(1,128)}, /*index=5*/f32[1,768]{1,0:T(1,128)}) custom-call(bf16[3,320,3072]{2,1,0:T(8,128)(2,1)} %get-tuple-element.46.gu_ref, bf16[768,3840]{1,0:T(8,128)(2,1)} %bitcast.59.wo_ref.u0.u1.u2.u3, ...), custom_call_target="tpu_custom_call" | custom-call | flops 5662310400 | bytes 16253952 | tf_op jit(solution)/shard_map/pallas_call | solution.py:309
  262.4 6.9 %bitcast_convert_fusion.1 = bf16[768,3072]{1,0:T(8,128)(2,1)} fusion(bf16[3,320,768]{2,1,0:T(8,128)(2,1)S(1)} %copy-done.27, bf16[3,320,3072]{2,1,0:T(8,128)(2,1)S(1)} %bitcast.315), kind=kOutput, calls=%fused_computation.1 | convolution fusion | flops 4532207616 | bytes 12091392 | tf_op jit(solution)/shard_map/snd,sne->de/dot_general | solution.py:321
  269.2 24.3 %shard_map.293 = (bf16[3,320,2304]{2,1,0:T(8,128)(2,1)}, f32[1,768]{1,0:T(1,128)}, f32[1,768]{1,0:T(1,128)}) custom-call(bf16[3,320,2304]{2,1,0:T(8,128)(2,1)} %get-tuple-element.45.qkv_ref, bf16[3,320,768]{2,1,0:T(8,128)(2,1)} %get-tuple-element.48.go_ref, bf16[3,12,320,320]{3,2,1,0:T(8,128)(2,1)} %get-tuple-element.49.p_ref), custom_call_target="tpu_custom_call" | custom-call | flops 7549747200 | bytes 17700864 | tf_op jit(solution)/shard_map/pallas_call | solution.py:309
  293.5 6.3 %bitcast_convert_fusion.2 = bf16[768,2304]{1,0:T(8,128)(2,1)S(1)} fusion(bf16[3,320,768]{2,1,0:T(8,128)(2,1)S(1)} %copy-done.25, bf16[3,320,2304]{2,1,0:T(8,128)(2,1)} %get-tuple-element.50.g_ref), kind=kOutput, calls=%fused_computation.2 | convolution fusion | flops 3399155712 | bytes 9437184 | tf_op jit(solution)/shard_map/snd,sne->de/dot_general | solution.py:321
  305.2 9.6 %shard_map.294 = (bf16[3,320,768]{2,1,0:T(8,128)(2,1)}, f32[1,768]{1,0:T(1,128)}, f32[1,768]{1,0:T(1,128)}) custom-call(bf16[3,320,2304]{2,1,0:T(8,128)(2,1)} %get-tuple-element.50.g_ref, bf16[768,2432]{1,0:T(8,128)(2,1)} %bitcast.312, bf16[3,320,768]{2,1,0:T(8,128)(2,1)} %pad_maximum_fusion.x_ref, f32[3,320,768]{2,1,0:T(8,128)} %get-tuple-element.51.gx_ref, ...), custom_call_target="tpu_custom_call" | custom-call | flops 3397386240 | bytes 14088192 | tf_op jit(solution)/shard_map/pallas_call | solution.py:309
  321.8 3.3 dynamic-slice_bitcast_fusion.1
  327.0 4.6 %collective-permute-done.34 = bf16[3,80,768]{2,1,0:T(8,128)(2,1)S(1)} collective-permute-done((bf16[3,80,768]{2,1,0:T(8,128)(2,1)S(1)}, bf16[3,80,768]{2,1,0:T(8,128)(2,1)S(1)}, u32[]{:S(2)}, u32[]{:S(2)}) %collective-permute-start.34) | collective-permute-done | bytes 368672 | tf_op jit(solution)/shard_map/ppermute | solution.py:33
  331.6 6.1 %collective-permute-done.35 = bf16[3,80,768]{2,1,0:T(8,128)(2,1)S(1)} collective-permute-done((bf16[3,80,768]{2,1,0:T(8,128)(2,1)S(1)}, bf16[3,80,768]{2,1,0:T(8,128)(2,1)S(1)}, u32[]{:S(2)}, u32[]{:S(2)}) %collective-permute-start.35) | collective-permute-done | bytes 368672 | tf_op jit(solution)/shard_map/ppermute | solution.py:33
  339.3 4.2 collective-permute-done.37
  345.3 6.2 %collective-permute-done.31 = bf16[3,80,768]{2,1,0:T(8,128)(2,1)S(1)} collective-permute-done((bf16[3,80,768]{2,1,0:T(8,128)(2,1)S(1)}, bf16[3,80,768]{2,1,0:T(8,128)(2,1)S(1)}, u32[]{:S(2)}, u32[]{:S(2)}) %collective-permute-start.31) | collective-permute-done | bytes 368672 | tf_op jit(solution)/shard_map/ppermute | solution.py:33
  353.8 4.5 %collective-permute-done.32 = bf16[3,80,768]{2,1,0:T(8,128)(2,1)S(1)} collective-permute-done((bf16[3,80,768]{2,1,0:T(8,128)(2,1)S(1)}, bf16[3,80,768]{2,1,0:T(8,128)(2,1)S(1)}, u32[]{:S(2)}, u32[]{:S(2)}) %collective-permute-start.32) | collective-permute-done | bytes 368672 | tf_op jit(solution)/shard_map/ppermute | solution.py:33
  361.8 3.6 collective-permute-start.48
  378.7 5.3 %collective-permute-done.43 = bf16[2,4,24,2304]{3,2,1,0:T(8,128)(2,1)S(1)} collective-permute-done((bf16[2,4,24,2304]{3,2,1,0:T(8,128)(2,1)S(1)}, bf16[2,4,24,2304]{3,2,1,0:T(8,128)(2,1)S(1)}, u32[]{:S(2)}, u32[]{:S(2)}) %collective-permute-start.43) | collective-permute-done | bytes 884768 | tf_op jit(solution)/shard_map/ppermute | solution.py:53
  387.6 9.8 %collective-permute-done.44 = bf16[4,24,2304]{2,1,0:T(8,128)(2,1)S(1)} collective-permute-done((bf16[4,24,2304]{2,1,0:T(8,128)(2,1)S(1)}, bf16[4,24,2304]{2,1,0:T(8,128)(2,1)S(1)}, u32[]{:S(2)}, u32[]{:S(2)}) %collective-permute-start.44) | collective-permute-done | bytes 442400 | tf_op jit(solution)/shard_map/ppermute | solution.py:53
  403.9 16.4 %collective-permute-done.49 = bf16[2,4,24,3072]{3,2,1,0:T(8,128)(2,1)S(1)} collective-permute-done((bf16[2,4,24,3072]{3,2,1,0:T(8,128)(2,1)S(1)}, bf16[2,4,24,3072]{3,2,1,0:T(8,128)(2,1)S(1)}, u32[]{:S(2)}, u32[]{:S(2)}) %collective-permute-start.49) | collective-permute-done | bytes 1179680 | tf_op jit(solution)/shard_map/ppermute | solution.py:53
  439.7 10.4 %collective-permute-done.52 = bf16[24,3072]{1,0:T(8,128)(2,1)S(1)} collective-permute-done((bf16[24,3072]{1,0:T(8,128)(2,1)S(1)}, bf16[24,3072]{1,0:T(8,128)(2,1)S(1)}, u32[]{:S(2)}, u32[]{:S(2)}) %collective-permute-start.52) | collective-permute-done | bytes 147488 | tf_op jit(solution)/shard_map/ppermute | solution.py:33
  (321 shorter events, 155.8 us)
Async XLA Ops:
  3.7 59.7 %collective-permute-start.13 = (bf16[24,3840]{1,0:T(8,128)(2,1)}, bf16[24,3840]{1,0:T(8,128)(2,1)}, u32[]{:S(2)}, u32[]{:S(2)}) collective-permute-start(bf16[24,3840]{1,0:T(8,128)(2,1)} %constant_dynamic-update-slice_fusion.6), channel_id=1, source_target_pairs={{0,2},{1,3},{2,0},{3,1},{4,6},{5,7},{6,4},{7,5},{8,10},{9,11},{10,... | collective-permute-start | bytes 552968 | tf_op jit(solution)/shard_map/ppermute | solution.py:33
  6.7 58.3 %collective-permute-start.14 = (bf16[24,3840]{1,0:T(8,128)(2,1)}, bf16[24,3840]{1,0:T(8,128)(2,1)}, u32[]{:S(2)}, u32[]{:S(2)}) collective-permute-start(bf16[24,3840]{1,0:T(8,128)(2,1)} %constant_dynamic-update-slice_fusion.6), channel_id=1, source_target_pairs={{0,4},{1,5},{2,6},{3,7},{4,0},{5,1},{6,2},{7,3},{8,12},{9,13},{10,... | collective-permute-start | bytes 552968 | tf_op jit(solution)/shard_map/ppermute | solution.py:33
  11.0 16.4 %collective-permute-start.10 = (s32[3,80]{1,0:T(4,128)S(1)}, s32[3,80]{1,0:T(4,128)S(1)}, u32[]{:S(2)}, u32[]{:S(2)}) collective-permute-start(s32[3,80]{1,0:T(4,128)S(1)} %get-tuple-element.122), channel_id=1, source_target_pairs={{0,8},{1,9},{2,10},{3,11},{4,12},{5,13},{6,14},{7,15},{8,0},{9,1},... | collective-permute-start | bytes 2888 | tf_op jit(solution)/shard_map/ppermute | solution.py:33
  11.1 16.5 %collective-permute-start.11 = (s32[3,80]{1,0:T(4,128)S(1)}, s32[3,80]{1,0:T(4,128)S(1)}, u32[]{:S(2)}, u32[]{:S(2)}) collective-permute-start(s32[3,80]{1,0:T(4,128)S(1)} %get-tuple-element.121), channel_id=1, source_target_pairs={{0,16},{1,17},{2,18},{3,19},{4,20},{5,21},{6,22},{7,23},{8,24},{9,... | collective-permute-start | bytes 2888 | tf_op jit(solution)/shard_map/ppermute | solution.py:33
  27.4 38.9 %collective-permute-start.15 = (bf16[24,3840]{1,0:T(8,128)(2,1)}, bf16[24,3840]{1,0:T(8,128)(2,1)}, u32[]{:S(2)}, u32[]{:S(2)}) collective-permute-start(bf16[24,3840]{1,0:T(8,128)(2,1)} %constant_dynamic-update-slice_fusion.6), channel_id=1, source_target_pairs={{0,6},{1,7},{2,4},{3,5},{4,2},{5,3},{6,0},{7,1},{8,14},{9,15},{10,... | collective-permute-start | bytes 552968 | tf_op jit(solution)/shard_map/ppermute | solution.py:33
  28.7 17.9 %collective-permute-start.4 = (bf16[24,2432]{1,0:T(8,128)(2,1)}, bf16[24,2432]{1,0:T(8,128)(2,1)}, u32[]{:S(2)}, u32[]{:S(2)}) collective-permute-start(bf16[24,2432]{1,0:T(8,128)(2,1)} %fusion.36), channel_id=1, source_target_pairs={{0,4},{1,5},{2,6},{3,7},{4,0},{5,1},{6,2},{7,3},{8,12},{9,13},{10,... | collective-permute-start | bytes 350216 | tf_op jit(solution)/shard_map/ppermute | solution.py:33
  65.0 17.4 %collective-permute-start.27 = (bf16[3,80,768]{2,1,0:T(8,128)(2,1)S(1)}, bf16[3,80,768]{2,1,0:T(8,128)(2,1)S(1)}, u32[]{:S(2)}, u32[]{:S(2)}) collective-permute-start(bf16[3,80,768]{2,1,0:T(8,128)(2,1)S(1)} %copy-done.11), channel_id=1, source_target_pairs={{0,8},{1,9},{2,10},{3,11},{4,12},{5,13},{6,14},{7,15},{8,0},{9,1},... | collective-permute-start | bytes 1105928 | tf_op jit(solution)/shard_map/ppermute | solution.py:33
  66.3 22.1 %collective-permute-start.28 = (bf16[3,80,768]{2,1,0:T(8,128)(2,1)S(1)}, bf16[3,80,768]{2,1,0:T(8,128)(2,1)S(1)}, u32[]{:S(2)}, u32[]{:S(2)}) collective-permute-start(bf16[3,80,768]{2,1,0:T(8,128)(2,1)S(1)} %copy-done.10), channel_id=1, source_target_pairs={{0,16},{1,17},{2,18},{3,19},{4,20},{5,21},{6,22},{7,23},{8,24},{9,... | collective-permute-start | bytes 1105928 | tf_op jit(solution)/shard_map/ppermute | solution.py:33
  68.8 26.7 %collective-permute-start.29 = (bf16[3,80,768]{2,1,0:T(8,128)(2,1)S(1)}, bf16[3,80,768]{2,1,0:T(8,128)(2,1)S(1)}, u32[]{:S(2)}, u32[]{:S(2)}) collective-permute-start(bf16[3,80,768]{2,1,0:T(8,128)(2,1)S(1)} %get-tuple-element.95), channel_id=1, source_target_pairs={{0,24},{1,25},{2,26},{3,27},{4,28},{5,29},{6,30},{7,31},{8,16},{9,... | collective-permute-start | bytes 1105928 | tf_op jit(solution)/shard_map/ppermute | solution.py:33
  72.6 29.4 %collective-permute-start.6 = (bf16[4,24,2432]{2,1,0:T(8,128)(2,1)S(1)}, bf16[4,24,2432]{2,1,0:T(8,128)(2,1)S(1)}, u32[]{:S(2)}, u32[]{:S(2)}) collective-permute-start(bf16[4,24,2432]{2,1,0:T(8,128)(2,1)S(1)} %bitcast_dynamic-update-slice_fusion.14), channel_id=1, source_target_pairs={{0,16},{1,17},{2,18},{3,19},{4,20},{5,21},{6,22},{7,23},{8,9},{9,8... | collective-permute-start | bytes 1400840 | tf_op jit(solution)/shard_map/ppermute | solution.py:53
  79.7 34.9 %collective-permute-start.23 = (bf16[4,96,768]{2,1,0:T(8,128)(2,1)S(1)}, bf16[4,96,768]{2,1,0:T(8,128)(2,1)S(1)}, u32[]{:S(2)}, u32[]{:S(2)}) collective-permute-start(bf16[4,96,768]{2,1,0:T(8,128)(2,1)S(1)} %bitcast_dynamic-update-slice_fusion.10), channel_id=1, source_target_pairs={{0,16},{1,17},{2,18},{3,19},{4,20},{5,21},{6,22},{7,23},{8,9},{9,8... | collective-permute-start | bytes 1769480 | tf_op jit(solution)/shard_map/ppermute | solution.py:53
  82.4 48.0 %collective-permute-start.16 = (bf16[4,24,3840]{2,1,0:T(8,128)(2,1)S(1)}, bf16[4,24,3840]{2,1,0:T(8,128)(2,1)S(1)}, u32[]{:S(2)}, u32[]{:S(2)}) collective-permute-start(bf16[4,24,3840]{2,1,0:T(8,128)(2,1)S(1)} %bitcast_dynamic-update-slice_fusion.6), channel_id=1, source_target_pairs={{0,16},{1,17},{2,18},{3,19},{4,20},{5,21},{6,22},{7,23},{8,9},{9,8... | collective-permute-start | bytes 2211848 | tf_op jit(solution)/shard_map/ppermute | solution.py:53
  102.1 31.0 %collective-permute-start.7 = (bf16[2,4,24,2432]{3,2,1,0:T(8,128)(2,1)S(1)}, bf16[2,4,24,2432]{3,2,1,0:T(8,128)(2,1)S(1)}, u32[]{:S(2)}, u32[]{:S(2)}) collective-permute-start(bf16[2,4,24,2432]{3,2,1,0:T(8,128)(2,1)S(1)} %pad_maximum_fusion.7), channel_id=1, source_target_pairs={{0,1},{1,0},{2,3},{3,2},{4,5},{5,4},{6,7},{7,6},{8,24},{9,25},{10,... | collective-permute-start | bytes 2801672 | tf_op jit(solution)/shard_map/ppermute | solution.py:53
  103.7 29.5 %collective-permute-start.8 = (bf16[2,4,24,2432]{3,2,1,0:T(8,128)(2,1)S(1)}, bf16[2,4,24,2432]{3,2,1,0:T(8,128)(2,1)S(1)}, u32[]{:S(2)}, u32[]{:S(2)}) collective-permute-start(bf16[2,4,24,2432]{3,2,1,0:T(8,128)(2,1)S(1)} %pad_maximum_fusion.7), channel_id=1, source_target_pairs={{0,8},{1,9},{2,10},{3,11},{4,12},{5,13},{6,14},{7,15},{8,0},{9,1},... | collective-permute-start | bytes 2801672 | tf_op jit(solution)/shard_map/ppermute | solution.py:33
  114.7 19.1 %collective-permute-start.24 = (bf16[2,4,96,768]{3,2,1,0:T(8,128)(2,1)S(1)}, bf16[2,4,96,768]{3,2,1,0:T(8,128)(2,1)}, u32[]{:S(2)}, u32[]{:S(2)}) collective-permute-start(bf16[2,4,96,768]{3,2,1,0:T(8,128)(2,1)S(1)} %pad_maximum_fusion.4), channel_id=1, source_target_pairs={{0,1},{1,0},{2,3},{3,2},{4,5},{5,4},{6,7},{7,6},{8,24},{9,25},{10,... | collective-permute-start | bytes 3538952 | tf_op jit(solution)/shard_map/ppermute | solution.py:53
  116.3 23.8 %collective-permute-start.25 = (bf16[2,4,96,768]{3,2,1,0:T(8,128)(2,1)S(1)}, bf16[2,4,96,768]{3,2,1,0:T(8,128)(2,1)S(1)}, u32[]{:S(2)}, u32[]{:S(2)}) collective-permute-start(bf16[2,4,96,768]{3,2,1,0:T(8,128)(2,1)S(1)} %pad_maximum_fusion.4), channel_id=1, source_target_pairs={{0,8},{1,9},{2,10},{3,11},{4,12},{5,13},{6,14},{7,15},{8,0},{9,1},... | collective-permute-start | bytes 3538952 | tf_op jit(solution)/shard_map/ppermute | solution.py:33
  130.6 19.4 %collective-permute-start.17 = (bf16[2,4,24,3840]{3,2,1,0:T(8,128)(2,1)S(1)}, bf16[2,4,24,3840]{3,2,1,0:T(8,128)(2,1)S(1)}, u32[]{:S(2)}, u32[]{:S(2)}) collective-permute-start(bf16[2,4,24,3840]{3,2,1,0:T(8,128)(2,1)S(1)} %pad_maximum_fusion.1), channel_id=1, source_target_pairs={{0,1},{1,0},{2,3},{3,2},{4,5},{5,4},{6,7},{7,6},{8,24},{9,25},{10,... | collective-permute-start | bytes 4423688 | tf_op jit(solution)/shard_map/ppermute | solution.py:53
  133.1 22.2 %collective-permute-start.18 = (bf16[2,4,24,3840]{3,2,1,0:T(8,128)(2,1)S(1)}, bf16[2,4,24,3840]{3,2,1,0:T(8,128)(2,1)S(1)}, u32[]{:S(2)}, u32[]{:S(2)}) collective-permute-start(bf16[2,4,24,3840]{3,2,1,0:T(8,128)(2,1)S(1)} %pad_maximum_fusion.1), channel_id=1, source_target_pairs={{0,8},{1,9},{2,10},{3,11},{4,12},{5,13},{6,14},{7,15},{8,0},{9,1},... | collective-permute-start | bytes 4423688 | tf_op jit(solution)/shard_map/ppermute | solution.py:33
  133.2 23.9 %collective-permute-start.9 = (bf16[2,4,24,2432]{3,2,1,0:T(8,128)(2,1)S(1)}, bf16[2,4,24,2432]{3,2,1,0:T(8,128)(2,1)S(1)}, u32[]{:S(2)}, u32[]{:S(2)}) collective-permute-start(bf16[2,4,24,2432]{3,2,1,0:T(8,128)(2,1)S(1)} %collective-permute-done.7), channel_id=1, source_target_pairs={{0,8},{1,9},{2,10},{3,11},{4,12},{5,13},{6,14},{7,15},{8,0},{9,1},... | collective-permute-start | bytes 2801672 | tf_op jit(solution)/shard_map/ppermute | solution.py:33
  133.9 52.0 %collective-permute-start.26 = (bf16[2,4,96,768]{3,2,1,0:T(8,128)(2,1)}, bf16[2,4,96,768]{3,2,1,0:T(8,128)(2,1)}, u32[]{:S(2)}, u32[]{:S(2)}) collective-permute-start(bf16[2,4,96,768]{3,2,1,0:T(8,128)(2,1)} %collective-permute-done.24), channel_id=1, source_target_pairs={{0,8},{1,9},{2,10},{3,11},{4,12},{5,13},{6,14},{7,15},{8,0},{9,1},... | collective-permute-start | bytes 3538952 | tf_op jit(solution)/shard_map/ppermute | solution.py:33
  150.0 39.7 %collective-permute-start.19 = (bf16[2,4,24,3840]{3,2,1,0:T(8,128)(2,1)S(1)}, bf16[2,4,24,3840]{3,2,1,0:T(8,128)(2,1)S(1)}, u32[]{:S(2)}, u32[]{:S(2)}) collective-permute-start(bf16[2,4,24,3840]{3,2,1,0:T(8,128)(2,1)S(1)} %collective-permute-done.17), channel_id=1, source_target_pairs={{0,8},{1,9},{2,10},{3,11},{4,12},{5,13},{6,14},{7,15},{8,0},{9,1},... | collective-permute-start | bytes 4423688 | tf_op jit(solution)/shard_map/ppermute | solution.py:33
  246.3 126.1 %collective-permute-start.54 = (bf16[2,4,2,96,768]{4,3,2,1,0:T(8,128)(2,1)}, bf16[2,4,2,96,768]{4,3,2,1,0:T(8,128)(2,1)}, u32[]{:S(2)}, u32[]{:S(2)}) collective-permute-start(bf16[2,4,2,96,768]{4,3,2,1,0:T(8,128)(2,1)} %dynamic-slice_bitcast_fusion), channel_id=1, source_target_pairs={{0,8},{1,9},{2,10},{3,11},{4,12},{5,13},{6,14},{7,15},{8,0},{9,1},... | collective-permute-start | bytes 7077896 | tf_op jit(solution)/shard_map/ppermute | solution.py:33
  301.3 67.4 %collective-permute-start.42 = (bf16[2,4,2,24,2304]{4,3,2,1,0:T(8,128)(2,1)}, bf16[2,4,2,24,2304]{4,3,2,1,0:T(8,128)(2,1)}, u32[]{:S(2)}, u32[]{:S(2)}) collective-permute-start(bf16[2,4,2,24,2304]{4,3,2,1,0:T(8,128)(2,1)} %dynamic-slice_bitcast_fusion.2), channel_id=1, source_target_pairs={{0,8},{1,9},{2,10},{3,11},{4,12},{5,13},{6,14},{7,15},{8,0},{9,1},... | collective-permute-start | bytes 5308424 | tf_op jit(solution)/shard_map/ppermute | solution.py:33
  326.2 17.3 %collective-permute-start.37 = (bf16[2,4,24,896]{3,2,1,0:T(8,128)(2,1)S(1)}, bf16[2,4,24,896]{3,2,1,0:T(8,128)(2,1)S(1)}, u32[]{:S(2)}, u32[]{:S(2)}) collective-permute-start(bf16[2,4,24,896]{3,2,1,0:T(8,128)(2,1)S(1)} %pad_maximum_fusion.9), channel_id=1, source_target_pairs={{0,16},{1,17},{2,18},{3,19},{4,20},{5,21},{6,22},{7,23},{8,9},{9,8... | collective-permute-start | bytes 1032200 | tf_op jit(solution)/shard_map/ppermute | solution.py:53
  375.1 26.9 %collective-permute-start.55 = (bf16[2,4,96,768]{3,2,1,0:T(8,128)(2,1)S(1)}, bf16[2,4,96,768]{3,2,1,0:T(8,128)(2,1)S(1)}, u32[]{:S(2)}, u32[]{:S(2)}) collective-permute-start(bf16[2,4,96,768]{3,2,1,0:T(8,128)(2,1)S(1)} %pad_maximum_fusion.6), channel_id=1, source_target_pairs={{0,16},{1,17},{2,18},{3,19},{4,20},{5,21},{6,22},{7,23},{8,9},{9,8... | collective-permute-start | bytes 3538952 | tf_op jit(solution)/shard_map/ppermute | solution.py:53
  386.0 34.3 %collective-permute-start.49 = (bf16[2,4,24,3072]{3,2,1,0:T(8,128)(2,1)S(1)}, bf16[2,4,24,3072]{3,2,1,0:T(8,128)(2,1)S(1)}, u32[]{:S(2)}, u32[]{:S(2)}) collective-permute-start(bf16[2,4,24,3072]{3,2,1,0:T(8,128)(2,1)S(1)} %pad_maximum_fusion.5), channel_id=1, source_target_pairs={{0,16},{1,17},{2,18},{3,19},{4,20},{5,21},{6,22},{7,23},{8,9},{9,8... | collective-permute-start | bytes 3538952 | tf_op jit(solution)/shard_map/ppermute | solution.py:53
  397.5 24.8 %collective-permute-start.45 = (bf16[24,2304]{1,0:T(8,128)(2,1)S(1)}, bf16[24,2304]{1,0:T(8,128)(2,1)S(1)}, u32[]{:S(2)}, u32[]{:S(2)}) collective-permute-start(bf16[24,2304]{1,0:T(8,128)(2,1)S(1)} %get-tuple-element.113), channel_id=1, source_target_pairs={{0,2},{1,3},{2,0},{3,1},{4,6},{5,7},{6,4},{7,5},{8,10},{9,11},{10,... | collective-permute-start | bytes 331784 | tf_op jit(solution)/shard_map/ppermute | solution.py:33
  397.6 24.7 %collective-permute-start.46 = (bf16[24,2304]{1,0:T(8,128)(2,1)S(1)}, bf16[24,2304]{1,0:T(8,128)(2,1)S(1)}, u32[]{:S(2)}, u32[]{:S(2)}) collective-permute-start(bf16[24,2304]{1,0:T(8,128)(2,1)S(1)} %get-tuple-element.115), channel_id=1, source_target_pairs={{0,4},{1,5},{2,6},{3,7},{4,0},{5,1},{6,2},{7,3},{8,12},{9,13},{10,... | collective-permute-start | bytes 331784 | tf_op jit(solution)/shard_map/ppermute | solution.py:33
  399.8 22.6 %collective-permute-start.47 = (bf16[24,2304]{1,0:T(8,128)(2,1)S(1)}, bf16[24,2304]{1,0:T(8,128)(2,1)S(1)}, u32[]{:S(2)}, u32[]{:S(2)}) collective-permute-start(bf16[24,2304]{1,0:T(8,128)(2,1)S(1)} %get-tuple-element.114), channel_id=1, source_target_pairs={{0,6},{1,7},{2,4},{3,5},{4,2},{5,3},{6,0},{7,1},{8,14},{9,15},{10,... | collective-permute-start | bytes 331784 | tf_op jit(solution)/shard_map/ppermute | solution.py:33
  402.3 20.7 %collective-permute-start.56 = (bf16[4,96,768]{2,1,0:T(8,128)(2,1)S(1)}, bf16[4,96,768]{2,1,0:T(8,128)(2,1)S(1)}, u32[]{:S(2)}, u32[]{:S(2)}) collective-permute-start(bf16[4,96,768]{2,1,0:T(8,128)(2,1)S(1)} %dynamic-slice_bitcast_fusion.4), channel_id=1, source_target_pairs={{0,1},{1,0},{2,3},{3,2},{4,5},{5,4},{6,7},{7,6},{8,24},{9,25},{10,... | collective-permute-start | bytes 1769480 | tf_op jit(solution)/shard_map/ppermute | solution.py:53
  431.0 19.1 %collective-permute-start.52 = (bf16[24,3072]{1,0:T(8,128)(2,1)S(1)}, bf16[24,3072]{1,0:T(8,128)(2,1)S(1)}, u32[]{:S(2)}, u32[]{:S(2)}) collective-permute-start(bf16[24,3072]{1,0:T(8,128)(2,1)S(1)} %get-tuple-element.110), channel_id=1, source_target_pairs={{0,4},{1,5},{2,6},{3,7},{4,0},{5,1},{6,2},{7,3},{8,12},{9,13},{10,... | collective-permute-start | bytes 442376 | tf_op jit(solution)/shard_map/ppermute | solution.py:33
  433.1 16.9 %collective-permute-start.53 = (bf16[24,3072]{1,0:T(8,128)(2,1)S(1)}, bf16[24,3072]{1,0:T(8,128)(2,1)S(1)}, u32[]{:S(2)}, u32[]{:S(2)}) collective-permute-start(bf16[24,3072]{1,0:T(8,128)(2,1)S(1)} %get-tuple-element.109), channel_id=1, source_target_pairs={{0,6},{1,7},{2,4},{3,5},{4,2},{5,3},{6,0},{7,1},{8,14},{9,15},{10,... | collective-permute-start | bytes 442376 | tf_op jit(solution)/shard_map/ppermute | solution.py:33
  (62 other events, 614.8 us)
